TPU v7x, 1024 devices: a whole 4x4x32 slice. The times are simulated.
1024 devices in a mesh: az: 256 (over y, x_lo, z), ht: 4 (over x_hi, core).
Axes of the slice: x: 4 (x_hi: 2, x_lo: 2; x = x_hi * 2 + x_lo), y: 4, z: 32, core: 2. Of those that a mesh axis runs over, the one named last changes fastest.
Arguments:
- right_side: float32 [64, 3072, 256], P('ht', 'az'), may hold values from -6 to 6
- base_coef: float32 [64, 3072, 256], P('ht', 'az'), may hold values from 0.3 to 3
- cell_type: int32 [64, 3072, 256], P('ht', 'az'), may hold values from 0 to 2
Outputs:
- pressure: float32 [64, 3072, 256], P('ht', 'az')
All inputs are finite; a program needn't handle non-finite values.
Results may differ from a plain program's by a relative error of at most 0.00002.
Values sent between devices are 32-bit elements; how exact they have to be, the bound alone decides.
A program may use at most 64 MiB of HBM per device.

v0:
```python
import jax
import jax.numpy as jnp
from jax import lax
from jax.sharding import PartitionSpec as P

DEGREE = 4
COARSE_SWEEPS = 6


shift_value = 0.002
smooth_low = 0.3
coarse_low = 0.02
high_end = 2.0


def extended_2(cells, sides, width):
    for axis, dim in sides:
        count = lax.axis_size(axis)
        head = lax.slice_in_dim(cells, 0, width, axis=dim)
        tail = lax.slice_in_dim(cells, cells.shape[dim] - width, cells.shape[dim], axis=dim)
        cells = jnp.concatenate(
            [
                lax.ppermute(tail, axis, [(i, (i + 1) % count) for i in range(count)]),
                cells,
                lax.ppermute(head, axis, [((i + 1) % count, i) for i in range(count)]),
            ],
            axis=dim,
        )
    return cells


def conductivity(base_coef, cell_type):
    factor = jnp.where(cell_type == 0, 0.1, jnp.where(cell_type == 1, 0.4, 1.0)).astype(jnp.float32)
    return base_coef * factor


def neighbours(values, coeffs):
    centre = values[1:-1, 1:-1]
    centre_coef = coeffs[1:-1, 1:-1]
    padded_field = jnp.pad(centre, ((0, 0), (0, 0), (1, 1)))
    padded_coef = jnp.pad(centre_coef, ((0, 0), (0, 0), (1, 1)))
    pairs = [
        (values[2:, 1:-1], coeffs[2:, 1:-1]),
        (values[:-2, 1:-1], coeffs[:-2, 1:-1]),
        (values[1:-1, 2:], coeffs[1:-1, 2:]),
        (values[1:-1, :-2], coeffs[1:-1, :-2]),
        (padded_field[:, :, 2:], padded_coef[:, :, 2:]),
        (padded_field[:, :, :-2], padded_coef[:, :, :-2]),
    ]
    return (centre, centre_coef, pairs)


def stencil(values, coeffs, spacing):
    centre, centre_coef, pairs = neighbours(values, coeffs)
    fluxes = jnp.zeros_like(centre)
    for value_next, coef_next in pairs:
        fluxes = fluxes + 0.5 * (centre_coef + coef_next) * (centre - value_next)
    return shift_value * centre + spacing * fluxes


def diagonal(coeffs, spacing):
    centre, centre_coef, pairs = neighbours(coeffs, coeffs)
    total = jnp.zeros_like(centre)
    for value_next, coef_next in pairs:
        total = total + 0.5 * (centre_coef + coef_next)
    return shift_value + spacing * total


def same(array):
    return array


def chebyshev(source, coeffs, pivots, inside, apply_op, shrink, degree, low_end, want_res):
    middle = 0.5 * (high_end + low_end)
    spread = 0.5 * (high_end - low_end)
    sigma_ratio = middle / spread
    rho_now = 1.0 / sigma_ratio
    direction = inside * source / pivots / middle
    iterate = direction
    for sweep_index in range(degree - 1):
        image = apply_op(iterate, coeffs)
        iterate, direction, source = (shrink(iterate), shrink(direction), shrink(source))
        coeffs, pivots, inside = (shrink(coeffs), shrink(pivots), shrink(inside))
        rho_next = 1.0 / (2.0 * sigma_ratio - rho_now)
        direction = inside * (
            rho_next * rho_now * direction + 2.0 * rho_next / spread * (source - image) / pivots
        )
        iterate = iterate + direction
        rho_now = rho_next
    residual = None
    if want_res:
        image = apply_op(iterate, coeffs)
        iterate = shrink(iterate)
        residual = shrink(source) - image
    return (iterate, residual)


def restrict(values):
    shape = values.shape
    blocks = values.reshape(shape[0] // 2, 2, shape[1] // 2, 2, shape[2] // 2, 2)
    return blocks.mean(axis=(1, 3, 5))


def prolong(values):
    return jnp.repeat(jnp.repeat(jnp.repeat(values, 2, 0), 2, 1), 2, 2)


def height_mask(rows, margin):
    position = lax.axis_index("ht") * rows - margin + jnp.arange(rows + 2 * margin, dtype=jnp.int32)
    inside = ((position >= 0) & (position < rows * lax.axis_size("ht"))).astype(jnp.float32)
    return inside[:, None, None]


def extend_fine(values):
    extended = extended_2(values, (("az", 1), ("ht", 0)), 1)
    return extended * height_mask(values.shape[0], 1)


def extend_coarse(values):
    extended = extended_2(values, (("az", 1), ("ht", 0)), 1)
    return extended * height_mask(values.shape[0], 1)


def single_level(source, coeffs, spacing, degree, low_end, want_res, extend):
    coef_ext = extend(coeffs)
    pivots = diagonal(coef_ext, spacing)

    def apply_op(iterate, coef_now):
        return stencil(extend(iterate), coef_now, spacing)

    return chebyshev(source, coef_ext, pivots, 1.0, apply_op, same, degree, low_end, want_res)


def on_device(right_side, base_coef, cell_type):
    kappa_fine = conductivity(base_coef, cell_type)
    fine_x, fine_r = single_level(
        right_side, kappa_fine, 1.0, DEGREE, smooth_low, True, extend_fine
    )
    middle_b = restrict(fine_r)
    kappa_mid = restrict(kappa_fine)
    middle_x, middle_r = single_level(
        middle_b, kappa_mid, 0.25, DEGREE, smooth_low, True, extend_fine
    )
    coarse_b = restrict(middle_r)
    kappa_coarse = restrict(kappa_mid)
    coarse_x, unused = single_level(
        coarse_b, kappa_coarse, 0.0625, COARSE_SWEEPS, coarse_low, False, extend_coarse
    )
    return fine_x + prolong(middle_x + prolong(coarse_x))


def solution(mesh):
    placed = (P("ht", "az", None), P("ht", "az", None), P("ht", "az", None))
    return jax.shard_map(
        on_device, mesh=mesh, in_specs=placed, out_specs=P("ht", "az", None), check_vma=False
    )
```

profile of v0, /device:TPU:1, one launch (start us, length us, event | category | flops | bytes accessed | tf_op | source)
XLA Modules:
  0.0 374.9 jit_solution(10047277628246221198)
XLA Ops:
  5.5 20.2 %collective-permute-start.1 = (f32[16,1,256]{2,0,1:T(8,128)S(1)}, f32[16,1,256]{2,0,1:T(8,128)S(1)}, u32[]{:S(2)}, u32[]{:S(2)}) collective-permute-start(f32[16,1,256]{2,0,1:T(8,128)S(1)} %get-tuple-element.61), channel_id=1, source_target_pairs={{4,0},{8,4},{12,8},{16,12},{20,16},{24,20},{28,24},{32,28},{36,32}... | collective-permute-start | bytes 49160 | tf_op jit(solution)/shard_map/ppermute | solution.py:25
  26.5 5.8 %collective-permute-start.2 = (f32[1,14,256]{2,0,1:T(1,128)S(1)}, f32[1,14,256]{2,0,1:T(1,128)S(1)}, u32[]{:S(2)}, u32[]{:S(2)}) collective-permute-start(f32[1,14,256]{2,0,1:T(1,128)S(1)} %get-tuple-element.50), channel_id=1, source_target_pairs={{0,1},{1,2},{2,3},{3,0},{4,5},{5,6},{6,7},{7,4},{8,9},{9,10},{10,1... | collective-permute-start | bytes 43016 | tf_op jit(solution)/shard_map/ppermute | solution.py:23
  34.3 4.6 %collective-permute-done.3 = f32[1,14,256]{2,0,1:T(1,128)S(1)} collective-permute-done((f32[1,14,256]{2,0,1:T(1,128)S(1)}, f32[1,14,256]{2,0,1:T(1,128)S(1)}, u32[]{:S(2)}, u32[]{:S(2)}) %collective-permute-start.3) | collective-permute-done | bytes 14368 | tf_op jit(solution)/shard_map/ppermute | solution.py:25
  41.1 7.6 %collective-permute-start.5 = (f32[16,1,256]{2,0,1:T(8,128)S(1)}, f32[16,1,256]{2,0,1:T(8,128)S(1)}, u32[]{:S(2)}, u32[]{:S(2)}) collective-permute-start(f32[16,1,256]{2,0,1:T(8,128)S(1)} %get-tuple-element.59), channel_id=1, source_target_pairs={{4,0},{8,4},{12,8},{16,12},{20,16},{24,20},{28,24},{32,28},{36,32}... | collective-permute-start | bytes 49160 | tf_op jit(solution)/shard_map/ppermute | solution.py:25
  54.9 14.0 %reshape.56 = f32[8,2,6,2,128,2]{5,4,1,0,3,2:T(8,128)} reshape(f32[16,12,256]{2,0,1:T(8,128)S(1)} %select_multiply_fusion) | data formatting | bytes 393216 | tf_op jit(solution)/shard_map/reshape | solution.py:100
  68.9 5.5 %reduce_sum.37 = f32[8,6,128]{2,0,1:T(8,128)S(1)} reduce(f32[8,2,6,2,128,2]{5,4,1,0,3,2:T(8,128)} %reshape.56, f32[]{:T(128)} %constant.46.clone.1), dimensions={1,3,5}, to_apply=%region_1.2 | reduce | flops 43008 | bytes 221188 | tf_op jit(solution)/shard_map/reduce_sum | solution.py:101
  76.8 7.6 %collective-permute-start.9 = (f32[16,1,256]{2,0,1:T(8,128)S(1)}, f32[16,1,256]{2,0,1:T(8,128)S(1)}, u32[]{:S(2)}, u32[]{:S(2)}) collective-permute-start(f32[16,1,256]{2,0,1:T(8,128)S(1)} %get-tuple-element.57), channel_id=1, source_target_pairs={{4,0},{8,4},{12,8},{16,12},{20,16},{24,20},{28,24},{32,28},{36,32}... | collective-permute-start | bytes 49160 | tf_op jit(solution)/shard_map/ppermute | solution.py:25
  85.3 6.6 %collective-permute-start.10 = (f32[1,14,256]{2,0,1:T(1,128)S(1)}, f32[1,14,256]{2,0,1:T(1,128)S(1)}, u32[]{:S(2)}, u32[]{:S(2)}) collective-permute-start(f32[1,14,256]{2,0,1:T(1,128)S(1)} %get-tuple-element.46), channel_id=1, source_target_pairs={{0,1},{1,2},{2,3},{3,0},{4,5},{5,6},{6,7},{7,4},{8,9},{9,10},{10,1... | collective-permute-start | bytes 43016 | tf_op jit(solution)/shard_map/ppermute | solution.py:23
  95.7 7.6 %collective-permute-start.21 = (f32[8,1,128]{2,0,1:T(8,128)S(1)}, f32[8,1,128]{2,0,1:T(8,128)S(1)}, u32[]{:S(2)}, u32[]{:S(2)}) collective-permute-start(f32[8,1,128]{2,0,1:T(8,128)S(1)} %get-tuple-element.81), channel_id=1, source_target_pairs={{4,0},{8,4},{12,8},{16,12},{20,16},{24,20},{28,24},{32,28},{36,32}... | collective-permute-start | bytes 12296 | tf_op jit(solution)/shard_map/ppermute | solution.py:25
  105.7 7.6 %collective-permute-start.13 = (f32[16,1,256]{2,0,1:T(8,128)S(1)}, f32[16,1,256]{2,0,1:T(8,128)S(1)}, u32[]{:S(2)}, u32[]{:S(2)}) collective-permute-start(f32[16,1,256]{2,0,1:T(8,128)S(1)} %get-tuple-element.55), channel_id=1, source_target_pairs={{4,0},{8,4},{12,8},{16,12},{20,16},{24,20},{28,24},{32,28},{36,32}... | collective-permute-start | bytes 49160 | tf_op jit(solution)/shard_map/ppermute | solution.py:25
  114.2 7.1 %collective-permute-start.14 = (f32[1,14,256]{2,0,1:T(1,128)S(1)}, f32[1,14,256]{2,0,1:T(1,128)S(1)}, u32[]{:S(2)}, u32[]{:S(2)}) collective-permute-start(f32[1,14,256]{2,0,1:T(1,128)S(1)} %get-tuple-element.44), channel_id=1, source_target_pairs={{0,1},{1,2},{2,3},{3,0},{4,5},{5,6},{6,7},{7,4},{8,9},{9,10},{10,1... | collective-permute-start | bytes 43016 | tf_op jit(solution)/shard_map/ppermute | solution.py:23
  123.3 5.1 %collective-permute-start.22 = (f32[1,8,128]{2,1,0:T(8,128)S(1)}, f32[1,8,128]{2,1,0:T(8,128)S(1)}, u32[]{:S(2)}, u32[]{:S(2)}) collective-permute-start(f32[1,8,128]{2,1,0:T(8,128)S(1)} %get-tuple-element.70), channel_id=1, source_target_pairs={{0,1},{1,2},{2,3},{3,0},{4,5},{5,6},{6,7},{7,4},{8,9},{9,10},{10,1... | collective-permute-start | bytes 12296 | tf_op jit(solution)/shard_map/ppermute | solution.py:23
  132.8 7.6 %collective-permute-start.17 = (f32[16,1,256]{2,0,1:T(8,128)S(1)}, f32[16,1,256]{2,0,1:T(8,128)S(1)}, u32[]{:S(2)}, u32[]{:S(2)}) collective-permute-start(f32[16,1,256]{2,0,1:T(8,128)S(1)} %get-tuple-element.53), channel_id=1, source_target_pairs={{4,0},{8,4},{12,8},{16,12},{20,16},{24,20},{28,24},{32,28},{36,32}... | collective-permute-start | bytes 49160 | tf_op jit(solution)/shard_map/ppermute | solution.py:25
  141.2 6.6 %collective-permute-start.18 = (f32[1,14,256]{2,0,1:T(1,128)S(1)}, f32[1,14,256]{2,0,1:T(1,128)S(1)}, u32[]{:S(2)}, u32[]{:S(2)}) collective-permute-start(f32[1,14,256]{2,0,1:T(1,128)S(1)} %get-tuple-element.42), channel_id=1, source_target_pairs={{0,1},{1,2},{2,3},{3,0},{4,5},{5,6},{6,7},{7,4},{8,9},{9,10},{10,1... | collective-permute-start | bytes 43016 | tf_op jit(solution)/shard_map/ppermute | solution.py:23
  149.8 4.5 %collective-permute-done.19 = f32[1,14,256]{2,0,1:T(1,128)S(1)} collective-permute-done((f32[1,14,256]{2,0,1:T(1,128)S(1)}, f32[1,14,256]{2,0,1:T(1,128)S(1)}, u32[]{:S(2)}, u32[]{:S(2)}) %collective-permute-start.19) | collective-permute-done | bytes 14368 | tf_op jit(solution)/shard_map/ppermute | solution.py:25
  154.7 14.0 %reshape.55 = f32[8,2,6,2,128,2]{5,4,1,0,3,2:T(8,128)} reshape(f32[16,12,256]{2,0,1:T(8,128)S(1)} %fusion.43) | data formatting | bytes 393216 | tf_op jit(solution)/shard_map/reshape | solution.py:100
  168.7 5.5 %reduce_sum.36 = f32[8,6,128]{2,0,1:T(8,128)S(1)} reduce(f32[8,2,6,2,128,2]{5,4,1,0,3,2:T(8,128)} %reshape.55, f32[]{:T(128)} %constant.46.clone.1), dimensions={1,3,5}, to_apply=%region_0.1 | reduce | flops 43008 | bytes 221188 | tf_op jit(solution)/shard_map/reduce_sum | solution.py:101
  176.2 7.6 %collective-permute-start.25 = (f32[8,1,128]{2,0,1:T(8,128)S(1)}, f32[8,1,128]{2,0,1:T(8,128)S(1)}, u32[]{:S(2)}, u32[]{:S(2)}) collective-permute-start(f32[8,1,128]{2,0,1:T(8,128)S(1)} %get-tuple-element.79), channel_id=1, source_target_pairs={{4,0},{8,4},{12,8},{16,12},{20,16},{24,20},{28,24},{32,28},{36,32}... | collective-permute-start | bytes 12296 | tf_op jit(solution)/shard_map/ppermute | solution.py:25
  189.8 4.5 %collective-permute-done.27 = f32[1,8,128]{2,1,0:T(8,128)S(1)} collective-permute-done((f32[1,8,128]{2,1,0:T(8,128)S(1)}, f32[1,8,128]{2,1,0:T(8,128)S(1)}, u32[]{:S(2)}, u32[]{:S(2)}) %collective-permute-start.27) | collective-permute-done | bytes 4128 | tf_op jit(solution)/shard_map/ppermute | solution.py:25
  196.5 7.6 %collective-permute-start.29 = (f32[8,1,128]{2,0,1:T(8,128)S(1)}, f32[8,1,128]{2,0,1:T(8,128)S(1)}, u32[]{:S(2)}, u32[]{:S(2)}) collective-permute-start(f32[8,1,128]{2,0,1:T(8,128)S(1)} %get-tuple-element.77), channel_id=1, source_target_pairs={{4,0},{8,4},{12,8},{16,12},{20,16},{24,20},{28,24},{32,28},{36,32}... | collective-permute-start | bytes 12296 | tf_op jit(solution)/shard_map/ppermute | solution.py:25
  210.6 4.5 %collective-permute-done.31 = f32[1,8,128]{2,1,0:T(8,128)S(1)} collective-permute-done((f32[1,8,128]{2,1,0:T(8,128)S(1)}, f32[1,8,128]{2,1,0:T(8,128)S(1)}, u32[]{:S(2)}, u32[]{:S(2)}) %collective-permute-start.31) | collective-permute-done | bytes 4128 | tf_op jit(solution)/shard_map/ppermute | solution.py:25
  217.2 7.6 %collective-permute-start.33 = (f32[8,1,128]{2,0,1:T(8,128)S(1)}, f32[8,1,128]{2,0,1:T(8,128)S(1)}, u32[]{:S(2)}, u32[]{:S(2)}) collective-permute-start(f32[8,1,128]{2,0,1:T(8,128)S(1)} %get-tuple-element.75), channel_id=1, source_target_pairs={{4,0},{8,4},{12,8},{16,12},{20,16},{24,20},{28,24},{32,28},{36,32}... | collective-permute-start | bytes 12296 | tf_op jit(solution)/shard_map/ppermute | solution.py:25
  226.8 7.6 %collective-permute-start.41 = (f32[4,1,64]{2,0,1:T(4,128)S(1)}, f32[4,1,64]{2,0,1:T(4,128)S(1)}, u32[]{:S(2)}, u32[]{:S(2)}) collective-permute-start(f32[4,1,64]{2,0,1:T(4,128)S(1)} %get-tuple-element.105), channel_id=1, source_target_pairs={{4,0},{8,4},{12,8},{16,12},{20,16},{24,20},{28,24},{32,28},{36,32}... | collective-permute-start | bytes 3080 | tf_op jit(solution)/shard_map/ppermute | solution.py:25
  239.4 4.5 %collective-permute-done.35 = f32[1,8,128]{2,1,0:T(8,128)S(1)} collective-permute-done((f32[1,8,128]{2,1,0:T(8,128)S(1)}, f32[1,8,128]{2,1,0:T(8,128)S(1)}, u32[]{:S(2)}, u32[]{:S(2)}) %collective-permute-start.35) | collective-permute-done | bytes 4128 | tf_op jit(solution)/shard_map/ppermute | solution.py:25
  246.1 7.6 %collective-permute-start.37 = (f32[8,1,128]{2,0,1:T(8,128)S(1)}, f32[8,1,128]{2,0,1:T(8,128)S(1)}, u32[]{:S(2)}, u32[]{:S(2)}) collective-permute-start(f32[8,1,128]{2,0,1:T(8,128)S(1)} %get-tuple-element.73), channel_id=1, source_target_pairs={{4,0},{8,4},{12,8},{16,12},{20,16},{24,20},{28,24},{32,28},{36,32}... | collective-permute-start | bytes 12296 | tf_op jit(solution)/shard_map/ppermute | solution.py:25
  258.2 5.1 %collective-permute-start.38 = (f32[1,8,128]{2,1,0:T(8,128)S(1)}, f32[1,8,128]{2,1,0:T(8,128)S(1)}, u32[]{:S(2)}, u32[]{:S(2)}) collective-permute-start(f32[1,8,128]{2,1,0:T(8,128)S(1)} %get-tuple-element.62), channel_id=1, source_target_pairs={{0,1},{1,2},{2,3},{3,0},{4,5},{5,6},{6,7},{7,4},{8,9},{9,10},{10,1... | collective-permute-start | bytes 12296 | tf_op jit(solution)/shard_map/ppermute | solution.py:23
  273.8 7.6 %collective-permute-start.45 = (f32[4,1,64]{2,0,1:T(4,128)S(1)}, f32[4,1,64]{2,0,1:T(4,128)S(1)}, u32[]{:S(2)}, u32[]{:S(2)}) collective-permute-start(f32[4,1,64]{2,0,1:T(4,128)S(1)} %get-tuple-element.103), channel_id=1, source_target_pairs={{4,0},{8,4},{12,8},{16,12},{20,16},{24,20},{28,24},{32,28},{36,32}... | collective-permute-start | bytes 3080 | tf_op jit(solution)/shard_map/ppermute | solution.py:25
  287.1 4.5 %collective-permute-done.47 = f32[1,5,64]{2,0,1:T(1,128)S(1)} collective-permute-done((f32[1,5,64]{2,0,1:T(1,128)S(1)}, f32[1,5,64]{2,0,1:T(1,128)S(1)}, u32[]{:S(2)}, u32[]{:S(2)}) %collective-permute-start.47) | collective-permute-done | bytes 1312 | tf_op jit(solution)/shard_map/ppermute | solution.py:25
  293.7 7.6 %collective-permute-start.49 = (f32[4,1,64]{2,0,1:T(4,128)S(1)}, f32[4,1,64]{2,0,1:T(4,128)S(1)}, u32[]{:S(2)}, u32[]{:S(2)}) collective-permute-start(f32[4,1,64]{2,0,1:T(4,128)S(1)} %get-tuple-element.101), channel_id=1, source_target_pairs={{4,0},{8,4},{12,8},{16,12},{20,16},{24,20},{28,24},{32,28},{36,32}... | collective-permute-start | bytes 3080 | tf_op jit(solution)/shard_map/ppermute | solution.py:25
  313.9 7.6 %collective-permute-start.53 = (f32[4,1,64]{2,0,1:T(4,128)S(1)}, f32[4,1,64]{2,0,1:T(4,128)S(1)}, u32[]{:S(2)}, u32[]{:S(2)}) collective-permute-start(f32[4,1,64]{2,0,1:T(4,128)S(1)} %get-tuple-element.99), channel_id=1, source_target_pairs={{4,0},{8,4},{12,8},{16,12},{20,16},{24,20},{28,24},{32,28},{36,32}... | collective-permute-start | bytes 3080 | tf_op jit(solution)/shard_map/ppermute | solution.py:25
  334.1 7.6 %collective-permute-start.57 = (f32[4,1,64]{2,0,1:T(4,128)S(1)}, f32[4,1,64]{2,0,1:T(4,128)S(1)}, u32[]{:S(2)}, u32[]{:S(2)}) collective-permute-start(f32[4,1,64]{2,0,1:T(4,128)S(1)} %get-tuple-element.97), channel_id=1, source_target_pairs={{4,0},{8,4},{12,8},{16,12},{20,16},{24,20},{28,24},{32,28},{36,32}... | collective-permute-start | bytes 3080 | tf_op jit(solution)/shard_map/ppermute | solution.py:25
  354.3 7.6 %collective-permute-start.61 = (f32[4,1,64]{2,0,1:T(4,128)S(1)}, f32[4,1,64]{2,0,1:T(4,128)S(1)}, u32[]{:S(2)}, u32[]{:S(2)}) collective-permute-start(f32[4,1,64]{2,0,1:T(4,128)S(1)} %get-tuple-element.95), channel_id=1, source_target_pairs={{4,0},{8,4},{12,8},{16,12},{20,16},{24,20},{28,24},{32,28},{36,32}... | collective-permute-start | bytes 3080 | tf_op jit(solution)/shard_map/ppermute | solution.py:25
  (214 shorter events, 137.4 us)
Async XLA Ops:
  1.1 24.6 %collective-permute-start = (f32[16,1,256]{2,0,1:T(8,128)S(1)}, f32[16,1,256]{2,0,1:T(8,128)S(1)}, u32[]{:S(2)}, u32[]{:S(2)}) collective-permute-start(f32[16,1,256]{2,0,1:T(8,128)S(1)} %get-tuple-element.60), channel_id=1, source_target_pairs={{0,4},{4,8},{8,12},{12,16},{16,20},{20,24},{24,28},{28,32},{32,36}... | collective-permute-start | bytes 49160 | tf_op jit(solution)/shard_map/ppermute | solution.py:23
  5.5 21.0 %collective-permute-start.1 = (f32[16,1,256]{2,0,1:T(8,128)S(1)}, f32[16,1,256]{2,0,1:T(8,128)S(1)}, u32[]{:S(2)}, u32[]{:S(2)}) collective-permute-start(f32[16,1,256]{2,0,1:T(8,128)S(1)} %get-tuple-element.61), channel_id=1, source_target_pairs={{4,0},{8,4},{12,8},{16,12},{20,16},{24,20},{28,24},{32,28},{36,32}... | collective-permute-start | bytes 49160 | tf_op jit(solution)/shard_map/ppermute | solution.py:25
  39.2 9.5 %collective-permute-start.4 = (f32[16,1,256]{2,0,1:T(8,128)S(1)}, f32[16,1,256]{2,0,1:T(8,128)S(1)}, u32[]{:S(2)}, u32[]{:S(2)}) collective-permute-start(f32[16,1,256]{2,0,1:T(8,128)S(1)} %get-tuple-element.58), channel_id=1, source_target_pairs={{0,4},{4,8},{8,12},{12,16},{16,20},{20,24},{24,28},{28,32},{32,36}... | collective-permute-start | bytes 49160 | tf_op jit(solution)/shard_map/ppermute | solution.py:23
  49.6 24.8 %collective-permute-start.6 = (f32[1,14,256]{2,0,1:T(1,128)S(1)}, f32[1,14,256]{2,0,1:T(1,128)S(1)}, u32[]{:S(2)}, u32[]{:S(2)}) collective-permute-start(f32[1,14,256]{2,0,1:T(1,128)S(1)} %get-tuple-element.48), channel_id=1, source_target_pairs={{0,1},{1,2},{2,3},{3,0},{4,5},{5,6},{6,7},{7,4},{8,9},{9,10},{10,1... | collective-permute-start | bytes 43016 | tf_op jit(solution)/shard_map/ppermute | solution.py:23
  53.0 21.4 %collective-permute-start.7 = (f32[1,14,256]{2,0,1:T(1,128)S(1)}, f32[1,14,256]{2,0,1:T(1,128)S(1)}, u32[]{:S(2)}, u32[]{:S(2)}) collective-permute-start(f32[1,14,256]{2,0,1:T(1,128)S(1)} %get-tuple-element.49), channel_id=1, source_target_pairs={{1,0},{2,1},{3,2},{0,3},{5,4},{6,5},{7,6},{4,7},{9,8},{10,9},{11,1... | collective-permute-start | bytes 43016 | tf_op jit(solution)/shard_map/ppermute | solution.py:25
  74.9 9.5 %collective-permute-start.8 = (f32[16,1,256]{2,0,1:T(8,128)S(1)}, f32[16,1,256]{2,0,1:T(8,128)S(1)}, u32[]{:S(2)}, u32[]{:S(2)}) collective-permute-start(f32[16,1,256]{2,0,1:T(8,128)S(1)} %get-tuple-element.56), channel_id=1, source_target_pairs={{0,4},{4,8},{8,12},{12,16},{16,20},{20,24},{24,28},{28,32},{32,36}... | collective-permute-start | bytes 49160 | tf_op jit(solution)/shard_map/ppermute | solution.py:23
  85.3 18.0 %collective-permute-start.10 = (f32[1,14,256]{2,0,1:T(1,128)S(1)}, f32[1,14,256]{2,0,1:T(1,128)S(1)}, u32[]{:S(2)}, u32[]{:S(2)}) collective-permute-start(f32[1,14,256]{2,0,1:T(1,128)S(1)} %get-tuple-element.46), channel_id=1, source_target_pairs={{0,1},{1,2},{2,3},{3,0},{4,5},{5,6},{6,7},{7,4},{8,9},{9,10},{10,1... | collective-permute-start | bytes 43016 | tf_op jit(solution)/shard_map/ppermute | solution.py:23
  91.8 11.5 %collective-permute-start.11 = (f32[1,14,256]{2,0,1:T(1,128)S(1)}, f32[1,14,256]{2,0,1:T(1,128)S(1)}, u32[]{:S(2)}, u32[]{:S(2)}) collective-permute-start(f32[1,14,256]{2,0,1:T(1,128)S(1)} %get-tuple-element.47), channel_id=1, source_target_pairs={{1,0},{2,1},{3,2},{0,3},{5,4},{6,5},{7,6},{4,7},{9,8},{10,9},{11,1... | collective-permute-start | bytes 43016 | tf_op jit(solution)/shard_map/ppermute | solution.py:25
  93.8 29.5 %collective-permute-start.20 = (f32[8,1,128]{2,0,1:T(8,128)S(1)}, f32[8,1,128]{2,0,1:T(8,128)S(1)}, u32[]{:S(2)}, u32[]{:S(2)}) collective-permute-start(f32[8,1,128]{2,0,1:T(8,128)S(1)} %get-tuple-element.80), channel_id=1, source_target_pairs={{0,4},{4,8},{8,12},{12,16},{16,20},{20,24},{24,28},{28,32},{32,36}... | collective-permute-start | bytes 12296 | tf_op jit(solution)/shard_map/ppermute | solution.py:23
  95.7 27.5 %collective-permute-start.21 = (f32[8,1,128]{2,0,1:T(8,128)S(1)}, f32[8,1,128]{2,0,1:T(8,128)S(1)}, u32[]{:S(2)}, u32[]{:S(2)}) collective-permute-start(f32[8,1,128]{2,0,1:T(8,128)S(1)} %get-tuple-element.81), channel_id=1, source_target_pairs={{4,0},{8,4},{12,8},{16,12},{20,16},{24,20},{28,24},{32,28},{36,32}... | collective-permute-start | bytes 12296 | tf_op jit(solution)/shard_map/ppermute | solution.py:25
  103.8 9.5 %collective-permute-start.12 = (f32[16,1,256]{2,0,1:T(8,128)S(1)}, f32[16,1,256]{2,0,1:T(8,128)S(1)}, u32[]{:S(2)}, u32[]{:S(2)}) collective-permute-start(f32[16,1,256]{2,0,1:T(8,128)S(1)} %get-tuple-element.54), channel_id=1, source_target_pairs={{0,4},{4,8},{8,12},{12,16},{16,20},{20,24},{24,28},{28,32},{32,36}... | collective-permute-start | bytes 49160 | tf_op jit(solution)/shard_map/ppermute | solution.py:23
  114.2 16.2 %collective-permute-start.14 = (f32[1,14,256]{2,0,1:T(1,128)S(1)}, f32[1,14,256]{2,0,1:T(1,128)S(1)}, u32[]{:S(2)}, u32[]{:S(2)}) collective-permute-start(f32[1,14,256]{2,0,1:T(1,128)S(1)} %get-tuple-element.44), channel_id=1, source_target_pairs={{0,1},{1,2},{2,3},{3,0},{4,5},{5,6},{6,7},{7,4},{8,9},{9,10},{10,1... | collective-permute-start | bytes 43016 | tf_op jit(solution)/shard_map/ppermute | solution.py:23
  121.3 9.1 %collective-permute-start.15 = (f32[1,14,256]{2,0,1:T(1,128)S(1)}, f32[1,14,256]{2,0,1:T(1,128)S(1)}, u32[]{:S(2)}, u32[]{:S(2)}) collective-permute-start(f32[1,14,256]{2,0,1:T(1,128)S(1)} %get-tuple-element.45), channel_id=1, source_target_pairs={{1,0},{2,1},{3,2},{0,3},{5,4},{6,5},{7,6},{4,7},{9,8},{10,9},{11,1... | collective-permute-start | bytes 43016 | tf_op jit(solution)/shard_map/ppermute | solution.py:25
  123.3 17.1 %collective-permute-start.22 = (f32[1,8,128]{2,1,0:T(8,128)S(1)}, f32[1,8,128]{2,1,0:T(8,128)S(1)}, u32[]{:S(2)}, u32[]{:S(2)}) collective-permute-start(f32[1,8,128]{2,1,0:T(8,128)S(1)} %get-tuple-element.70), channel_id=1, source_target_pairs={{0,1},{1,2},{2,3},{3,0},{4,5},{5,6},{6,7},{7,4},{8,9},{9,10},{10,1... | collective-permute-start | bytes 12296 | tf_op jit(solution)/shard_map/ppermute | solution.py:23
  128.4 12.0 %collective-permute-start.23 = (f32[1,8,128]{2,1,0:T(8,128)S(1)}, f32[1,8,128]{2,1,0:T(8,128)S(1)}, u32[]{:S(2)}, u32[]{:S(2)}) collective-permute-start(f32[1,8,128]{2,1,0:T(8,128)S(1)} %get-tuple-element.71), channel_id=1, source_target_pairs={{1,0},{2,1},{3,2},{0,3},{5,4},{6,5},{7,6},{4,7},{9,8},{10,9},{11,1... | collective-permute-start | bytes 12296 | tf_op jit(solution)/shard_map/ppermute | solution.py:25
  130.8 9.6 %collective-permute-start.16 = (f32[16,1,256]{2,0,1:T(8,128)S(1)}, f32[16,1,256]{2,0,1:T(8,128)S(1)}, u32[]{:S(2)}, u32[]{:S(2)}) collective-permute-start(f32[16,1,256]{2,0,1:T(8,128)S(1)} %get-tuple-element.52), channel_id=1, source_target_pairs={{0,4},{4,8},{8,12},{12,16},{16,20},{20,24},{24,28},{28,32},{32,36}... | collective-permute-start | bytes 49160 | tf_op jit(solution)/shard_map/ppermute | solution.py:23
  174.3 9.5 %collective-permute-start.24 = (f32[8,1,128]{2,0,1:T(8,128)S(1)}, f32[8,1,128]{2,0,1:T(8,128)S(1)}, u32[]{:S(2)}, u32[]{:S(2)}) collective-permute-start(f32[8,1,128]{2,0,1:T(8,128)S(1)} %get-tuple-element.78), channel_id=1, source_target_pairs={{0,4},{4,8},{8,12},{12,16},{16,20},{20,24},{24,28},{28,32},{32,36}... | collective-permute-start | bytes 12296 | tf_op jit(solution)/shard_map/ppermute | solution.py:23
  194.6 11.3 %collective-permute-start.28 = (f32[8,1,128]{2,0,1:T(8,128)S(1)}, f32[8,1,128]{2,0,1:T(8,128)S(1)}, u32[]{:S(2)}, u32[]{:S(2)}) collective-permute-start(f32[8,1,128]{2,0,1:T(8,128)S(1)} %get-tuple-element.76), channel_id=1, source_target_pairs={{0,4},{4,8},{8,12},{12,16},{16,20},{20,24},{24,28},{28,32},{32,36}... | collective-permute-start | bytes 12296 | tf_op jit(solution)/shard_map/ppermute | solution.py:23
  196.5 9.4 %collective-permute-start.29 = (f32[8,1,128]{2,0,1:T(8,128)S(1)}, f32[8,1,128]{2,0,1:T(8,128)S(1)}, u32[]{:S(2)}, u32[]{:S(2)}) collective-permute-start(f32[8,1,128]{2,0,1:T(8,128)S(1)} %get-tuple-element.77), channel_id=1, source_target_pairs={{4,0},{8,4},{12,8},{16,12},{20,16},{24,20},{28,24},{32,28},{36,32}... | collective-permute-start | bytes 12296 | tf_op jit(solution)/shard_map/ppermute | solution.py:25
  215.3 19.1 %collective-permute-start.32 = (f32[8,1,128]{2,0,1:T(8,128)S(1)}, f32[8,1,128]{2,0,1:T(8,128)S(1)}, u32[]{:S(2)}, u32[]{:S(2)}) collective-permute-start(f32[8,1,128]{2,0,1:T(8,128)S(1)} %get-tuple-element.74), channel_id=1, source_target_pairs={{0,4},{4,8},{8,12},{12,16},{16,20},{20,24},{24,28},{28,32},{32,36}... | collective-permute-start | bytes 12296 | tf_op jit(solution)/shard_map/ppermute | solution.py:23
  217.2 17.2 %collective-permute-start.33 = (f32[8,1,128]{2,0,1:T(8,128)S(1)}, f32[8,1,128]{2,0,1:T(8,128)S(1)}, u32[]{:S(2)}, u32[]{:S(2)}) collective-permute-start(f32[8,1,128]{2,0,1:T(8,128)S(1)} %get-tuple-element.75), channel_id=1, source_target_pairs={{4,0},{8,4},{12,8},{16,12},{20,16},{24,20},{28,24},{32,28},{36,32}... | collective-permute-start | bytes 12296 | tf_op jit(solution)/shard_map/ppermute | solution.py:25
  224.8 28.8 %collective-permute-start.40 = (f32[4,1,64]{2,0,1:T(4,128)S(1)}, f32[4,1,64]{2,0,1:T(4,128)S(1)}, u32[]{:S(2)}, u32[]{:S(2)}) collective-permute-start(f32[4,1,64]{2,0,1:T(4,128)S(1)} %get-tuple-element.104), channel_id=1, source_target_pairs={{0,4},{4,8},{8,12},{12,16},{16,20},{20,24},{24,28},{28,32},{32,36}... | collective-permute-start | bytes 3080 | tf_op jit(solution)/shard_map/ppermute | solution.py:23
  226.8 26.9 %collective-permute-start.41 = (f32[4,1,64]{2,0,1:T(4,128)S(1)}, f32[4,1,64]{2,0,1:T(4,128)S(1)}, u32[]{:S(2)}, u32[]{:S(2)}) collective-permute-start(f32[4,1,64]{2,0,1:T(4,128)S(1)} %get-tuple-element.105), channel_id=1, source_target_pairs={{4,0},{8,4},{12,8},{16,12},{20,16},{24,20},{28,24},{32,28},{36,32}... | collective-permute-start | bytes 3080 | tf_op jit(solution)/shard_map/ppermute | solution.py:25
  244.1 14.0 %collective-permute-start.36 = (f32[8,1,128]{2,0,1:T(8,128)S(1)}, f32[8,1,128]{2,0,1:T(8,128)S(1)}, u32[]{:S(2)}, u32[]{:S(2)}) collective-permute-start(f32[8,1,128]{2,0,1:T(8,128)S(1)} %get-tuple-element.72), channel_id=1, source_target_pairs={{0,4},{4,8},{8,12},{12,16},{16,20},{20,24},{24,28},{28,32},{32,36}... | collective-permute-start | bytes 12296 | tf_op jit(solution)/shard_map/ppermute | solution.py:23
  246.1 12.1 %collective-permute-start.37 = (f32[8,1,128]{2,0,1:T(8,128)S(1)}, f32[8,1,128]{2,0,1:T(8,128)S(1)}, u32[]{:S(2)}, u32[]{:S(2)}) collective-permute-start(f32[8,1,128]{2,0,1:T(8,128)S(1)} %get-tuple-element.73), channel_id=1, source_target_pairs={{4,0},{8,4},{12,8},{16,12},{20,16},{24,20},{28,24},{32,28},{36,32}... | collective-permute-start | bytes 12296 | tf_op jit(solution)/shard_map/ppermute | solution.py:25
  253.7 11.8 %collective-permute-start.42 = (f32[1,5,64]{2,0,1:T(1,128)S(1)}, f32[1,5,64]{2,0,1:T(1,128)S(1)}, u32[]{:S(2)}, u32[]{:S(2)}) collective-permute-start(f32[1,5,64]{2,0,1:T(1,128)S(1)} %get-tuple-element.92), channel_id=1, source_target_pairs={{0,1},{1,2},{2,3},{3,0},{4,5},{5,6},{6,7},{7,4},{8,9},{9,10},{10,1... | collective-permute-start | bytes 3848 | tf_op jit(solution)/shard_map/ppermute | solution.py:23
  256.2 9.3 %collective-permute-start.43 = (f32[1,5,64]{2,0,1:T(1,128)S(1)}, f32[1,5,64]{2,0,1:T(1,128)S(1)}, u32[]{:S(2)}, u32[]{:S(2)}) collective-permute-start(f32[1,5,64]{2,0,1:T(1,128)S(1)} %get-tuple-element.93), channel_id=1, source_target_pairs={{1,0},{2,1},{3,2},{0,3},{5,4},{6,5},{7,6},{4,7},{9,8},{10,9},{11,1... | collective-permute-start | bytes 3848 | tf_op jit(solution)/shard_map/ppermute | solution.py:25
  271.8 9.5 %collective-permute-start.44 = (f32[4,1,64]{2,0,1:T(4,128)S(1)}, f32[4,1,64]{2,0,1:T(4,128)S(1)}, u32[]{:S(2)}, u32[]{:S(2)}) collective-permute-start(f32[4,1,64]{2,0,1:T(4,128)S(1)} %get-tuple-element.102), channel_id=1, source_target_pairs={{0,4},{4,8},{8,12},{12,16},{16,20},{20,24},{24,28},{28,32},{32,36}... | collective-permute-start | bytes 3080 | tf_op jit(solution)/shard_map/ppermute | solution.py:23
  291.8 9.5 %collective-permute-start.48 = (f32[4,1,64]{2,0,1:T(4,128)S(1)}, f32[4,1,64]{2,0,1:T(4,128)S(1)}, u32[]{:S(2)}, u32[]{:S(2)}) collective-permute-start(f32[4,1,64]{2,0,1:T(4,128)S(1)} %get-tuple-element.100), channel_id=1, source_target_pairs={{0,4},{4,8},{8,12},{12,16},{16,20},{20,24},{24,28},{28,32},{32,36}... | collective-permute-start | bytes 3080 | tf_op jit(solution)/shard_map/ppermute | solution.py:23
  311.9 9.5 %collective-permute-start.52 = (f32[4,1,64]{2,0,1:T(4,128)S(1)}, f32[4,1,64]{2,0,1:T(4,128)S(1)}, u32[]{:S(2)}, u32[]{:S(2)}) collective-permute-start(f32[4,1,64]{2,0,1:T(4,128)S(1)} %get-tuple-element.98), channel_id=1, source_target_pairs={{0,4},{4,8},{8,12},{12,16},{16,20},{20,24},{24,28},{28,32},{32,36}... | collective-permute-start | bytes 3080 | tf_op jit(solution)/shard_map/ppermute | solution.py:23
  332.1 9.5 %collective-permute-start.56 = (f32[4,1,64]{2,0,1:T(4,128)S(1)}, f32[4,1,64]{2,0,1:T(4,128)S(1)}, u32[]{:S(2)}, u32[]{:S(2)}) collective-permute-start(f32[4,1,64]{2,0,1:T(4,128)S(1)} %get-tuple-element.96), channel_id=1, source_target_pairs={{0,4},{4,8},{8,12},{12,16},{16,20},{20,24},{24,28},{28,32},{32,36}... | collective-permute-start | bytes 3080 | tf_op jit(solution)/shard_map/ppermute | solution.py:23
  352.3 9.5 %collective-permute-start.60 = (f32[4,1,64]{2,0,1:T(4,128)S(1)}, f32[4,1,64]{2,0,1:T(4,128)S(1)}, u32[]{:S(2)}, u32[]{:S(2)}) collective-permute-start(f32[4,1,64]{2,0,1:T(4,128)S(1)} %get-tuple-element.94), channel_id=1, source_target_pairs={{0,4},{4,8},{8,12},{12,16},{16,20},{20,24},{24,28},{28,32},{32,36}... | collective-permute-start | bytes 3080 | tf_op jit(solution)/shard_map/ppermute | solution.py:23
  (33 other events, 258.3 us)
where the time goes:
time: 377 us; the launch traced here: 375 us
  starting transfers between devices  266 us (71%)
  waiting for transfers between devices  57.6 us (15%)
  local copies, waits for them, and re-layouts  32.9 us (9%)
  other arithmetic  17.2 us (5%)
    ppermute x32, starting transfers between devices, extended_2(): lax.ppermute(head, axis, [((i + 1) % count, i) for i in range(count)])  165 us
    ppermute x32, starting transfers between devices, extended_2(): lax.ppermute(tail, axis, [(i, (i + 1) % count) for i in range(count)])  101 us
    ppermute x32, waiting for transfers between devices, extended_2(): lax.ppermute(head, axis, [((i + 1) % count, i) for i in range(count)])  57.5 us
    reshape x3, local copies, waits for them, and re-layouts, restrict(): values.reshape(shape[0] // 2, 2, shape[1] // 2, 2, shape[2] // 2, 2)  29.5 us
    reduce_sum x4, other arithmetic, restrict(): return blocks.mean(axis=(1, 3, 5))  11.4 us
  transfers between devices with their start and end apart: 64, of which 22 were waited for; matrix products, arithmetic and copies ran while one was open for 6% of the time, Pallas kernels for 0%

commit v1 on v0

v1 whole, which is shorter than its diff:
```python
import functools

import jax
import jax.numpy as jnp
from jax import lax
from jax.experimental import pallas as pl
from jax.experimental.pallas import tpu as pltpu
from jax.sharding import PartitionSpec as P

DEGREE = 4
COARSE_SWEEPS = 6

shift_value = 0.002
smooth_low = 0.3
coarse_low = 0.02
high_end = 2.0

F32 = jnp.float32
BF16 = jnp.bfloat16
MESH = pl.DeviceIdType.MESH

SIDES = [(0, 1), (0, -1)]
ENDS = [(1, 0), (-1, 0)]
CORNERS = [(1, 1), (1, -1), (-1, 1), (-1, -1)]
NEAR = SIDES + ENDS + CORNERS
REACH = 2


def chebyshev_steps(degree, low_end):
    middle = 0.5 * (high_end + low_end)
    spread = 0.5 * (high_end - low_end)
    sigma_ratio = middle / spread
    rho_now = 1.0 / sigma_ratio
    steps = []
    for _ in range(degree - 1):
        rho_next = 1.0 / (2.0 * sigma_ratio - rho_now)
        steps.append((rho_next * rho_now, 2.0 * rho_next / spread))
        rho_now = rho_next
    return 1.0 / middle, steps


def exact_dot(values, weights):
    high = values.astype(BF16)
    rest = values - high.astype(F32)
    mid = rest.astype(BF16)
    low = (rest - mid.astype(F32)).astype(BF16)
    total = jnp.dot(high, weights, preferred_element_type=F32)
    total = total + jnp.dot(mid, weights, preferred_element_type=F32)
    return total + jnp.dot(low, weights, preferred_element_type=F32)


def each_row(start, count, block, body):
    def step(i, carry):
        for j in range(block):
            body(start + i * block + j)
        return carry

    lax.fori_loop(0, count // block, step, 0)


def next_in(values, axis):
    return pltpu.roll(values, values.shape[axis] - 1, axis)


def last_in(values, axis):
    return pltpu.roll(values, 1, axis)


def face_coefs(k, low, high, half, last_lane, first_lane):
    up = half * (k + high)
    down = half * (k + low)
    side = half * (k + next_in(k, 0))
    out = half * (k + jnp.where(last_lane, 0.0, next_in(k, 1)))
    back = jnp.where(first_lane, half * k, last_in(out, 1))
    pivots = shift_value + (up + down + side + last_in(side, 0) + out + back)
    return up, down, side, jnp.where(last_lane, 0.0, out), pivots


def in_layer(x, side, out):
    return (
        side * next_in(x, 0) + last_in(side * x, 0) + out * next_in(x, 1) + last_in(out * x, 1)
    )


class Level:
    def __init__(self, refs, spacing, low_end, degree):
        self.k, self.b, self.x, self.y, self.d, self.up, self.side, self.out, self.inv, self.piv = refs
        self.rows, self.sub, self.lanes = self.b.shape
        self.half = 0.5 * spacing
        self.first, self.steps = chebyshev_steps(degree, low_end)

    def set_up(self, begin, end, block):
        lane = lax.broadcasted_iota(jnp.int32, (self.sub, self.lanes), 1)
        last_lane, first_lane = lane == self.lanes - 1, lane == 0

        def body(h):
            up, _, side, out, piv = face_coefs(
                self.k[h + 1], self.k[h], self.k[h + 2], self.half, last_lane, first_lane
            )
            self.up[h], self.side[h], self.out[h], self.piv[h] = up, side, out, piv
            inside = jnp.where((h >= begin) & (h < end), 1.0, 0.0).astype(F32)
            self.inv[h] = inside / piv

        each_row(0, self.rows, block, body)

    def gathered(self, h):
        x = self.x[h]
        total = self.b[h] + self.up[h] * self.x[h + 1] + self.up[h - 1] * self.x[h - 1]
        return total + in_layer(x, self.side[h], self.out[h]), x

    def smooth(self, block):
        def start(h):
            self.x[h] = self.b[h] * self.inv[h] * self.first

        each_row(0, self.rows, block, start)
        for number, (keep, add) in enumerate(self.steps):

            def body(h):
                total, x = self.gathered(h)
                d = keep * (self.d[h] if number else x) + add * (total * self.inv[h] - x)
                self.d[h] = d
                self.y[h] = x + d

            each_row(number + 1, self.rows - 2 * (number + 1), block, body)
            self.x, self.y = self.y, self.x

    def residual(self, h):
        total, x = self.gathered(h)
        return total - self.piv[h] * x


def kernel(n_ht, n_az, rhs_hbm, coef_hbm, type_hbm, res_hbm, s):
    ht, az = lax.axis_index("ht"), lax.axis_index("az")
    has = {1: ht < n_ht - 1, -1: ht > 0}
    rows, cols, _ = rhs_hbm.shape

    def device(dh, da):
        return {"ht": ht + dh, "az": lax.rem(az + (da + n_az), n_az)}

    def there(dh, run):
        if dh == 0:
            run()
        else:
            pl.when(has[dh])(run)

    loads = [
        pltpu.make_async_copy(src, dst, s.load_sem.at[i])
        for i, (src, dst) in enumerate(
            [(coef_hbm, s.coef), (type_hbm, s.kind), (rhs_hbm, s.rhs)]
        )
    ]
    for load in loads:
        load.start()

    barrier = pltpu.get_barrier_semaphore()
    far = [
        (dh, da)
        for da in range(-REACH, REACH + 1)
        for dh in range(n_ht)
        if (dh, da) != (0, 0)
    ]

    def far_device(dh, da):
        return {"ht": lax.rem(ht + dh, n_ht), "az": lax.rem(az + (da + n_az), n_az)}

    for dh, da in far:
        pl.semaphore_signal(barrier, inc=1, device_id=far_device(dh, da), device_id_type=MESH)

    sent = []

    def copies(first_slot, directions, src, dst):
        made = []
        for i, (dh, da) in enumerate(directions):
            slot = first_slot + i
            copy = pltpu.make_async_remote_copy(
                src_ref=src(dh, da),
                dst_ref=dst(dh, da),
                send_sem=s.send_sem.at[slot],
                recv_sem=s.recv_sem.at[slot],
                device_id=device(dh, da),
                device_id_type=MESH,
            )
            there(dh, copy.start)
            made.append((dh, da, copy))
        sent.extend(made)
        return {(dh, da): copy for dh, da, copy in made}

    s.k0[...] = jnp.zeros_like(s.k0)
    s.b0[...] = jnp.zeros_like(s.b0)
    s.k1[...] = jnp.zeros_like(s.k1)
    s.b1[...] = jnp.zeros_like(s.b1)
    s.k2[...] = jnp.zeros_like(s.k2)
    s.b2[...] = jnp.zeros_like(s.b2)
    s.x2[...] = jnp.zeros_like(s.x2)
    s.y2[...] = jnp.zeros_like(s.y2)

    def iotas(shape):
        return lax.broadcasted_iota(jnp.int32, shape, 0), lax.broadcasted_iota(jnp.int32, shape, 1)

    def as_weights(picked, value):
        return jnp.where(picked, value, 0.0).astype(BF16)

    i, j = iotas(s.down0.shape)
    s.down0[...] = as_weights(i // 2 == j, 0.125)
    i, j = iotas(s.down1.shape)
    s.down1[...] = as_weights(i // 2 == j % 64, 0.125)
    i, j = iotas(s.wide1.shape)
    s.wide1[...] = as_weights(i == j // 2, 1.0)
    i, j = iotas(s.wide2a.shape)
    s.wide2a[...] = as_weights(i == j // 2, 1.0)
    s.wide2b[...] = as_weights(i == 64 + j // 2, 1.0)

    loads[0].wait()
    loads[1].wait()

    def conductivity(h):
        kind = s.kind[h]
        factor = jnp.where(kind == 0, 0.1, jnp.where(kind == 1, 0.4, 1.0)).astype(F32)
        kappa = s.coef[h] * factor
        s.kappa[h] = kappa
        s.k0[h + 5, 0:cols] = kappa
        s.k4_out[0, h] = kappa[cols - 4 : cols]
        s.k4_out[1, h] = kappa[0:4]
        s.k5_out[0, h] = kappa[cols - 5 : cols - 4]
        s.k5_out[1, h] = kappa[4:5]

    each_row(0, rows, 4, conductivity)
    pl.semaphore_wait(barrier, len(far))

    def pick(ref, dh, da, layers, size):
        side = 0 if da == 1 else 1
        if dh == 0:
            return ref.at[side]
        return ref.at[side, size - layers : size] if dh == 1 else ref.at[side, 0:layers]

    def layers_of(ref, dh, layers):
        size = ref.shape[0]
        return ref.at[size - layers : size] if dh == 1 else ref.at[0:layers]

    def end(dh):
        return 0 if dh == 1 else 1

    def corner(dh, da):
        return (0 if dh == 1 else 2) + (0 if da == 1 else 1)

    k4 = copies(0, SIDES, lambda dh, da: pick(s.k4_out, dh, da, 0, 0), lambda dh, da: s.k4_in.at[0 if da == 1 else 1])
    k5 = copies(2, SIDES, lambda dh, da: pick(s.k5_out, dh, da, 0, 0), lambda dh, da: s.k5_in.at[0 if da == 1 else 1])
    ke = copies(4, ENDS, lambda dh, da: layers_of(s.kappa, dh, 5), lambda dh, da: s.ke_in.at[end(dh)])
    kc = copies(6, CORNERS, lambda dh, da: pick(s.k4_out, dh, da, 4, rows), lambda dh, da: s.kc_in.at[corner(dh, da)])

    loads[2].wait()

    def source(h):
        rhs = s.rhs[h]
        s.b0[h + 4, 0:cols] = rhs
        s.b4_out[0, h] = rhs[cols - 4 : cols]
        s.b4_out[1, h] = rhs[0:4]

    each_row(0, rows, 4, source)
    b4 = copies(10, SIDES, lambda dh, da: pick(s.b4_out, dh, da, 0, 0), lambda dh, da: s.b4_in.at[0 if da == 1 else 1])
    be = copies(12, ENDS, lambda dh, da: layers_of(s.rhs, dh, 4), lambda dh, da: s.be_in.at[end(dh)])
    bc = copies(14, CORNERS, lambda dh, da: pick(s.b4_out, dh, da, 3, rows), lambda dh, da: s.bc_in.at[corner(dh, da)])

    mid_rows, mid_cols = rows // 2, cols // 2

    def restrict0(pair_sum):
        each_row(0, mid_rows, 4, pair_sum)
        s.halves[...] = exact_dot(s.pairs[...].reshape(mid_rows * 16, -1), s.down0[...])
        count = mid_rows * 8
        means = s.halves[pl.ds(0, count, stride=2), :] + s.halves[pl.ds(1, count, stride=2), :]
        return means.reshape(mid_rows, 8, -1)

    def restrict1(values):
        parts = [values[2 * i] + values[2 * i + 1] for i in range(mid_rows // 2)]
        s.quarters[...] = exact_dot(jnp.concatenate(parts, axis=0), s.down1[...])
        means = s.quarters[pl.ds(0, 16, stride=2), :] + s.quarters[pl.ds(1, 16, stride=2), :]
        lane = lax.broadcasted_iota(jnp.int32, (8, 128), 1)
        return jnp.where(lane < 64, means[0:8], means[8:16])

    def pair_of_kappa(i):
        s.pairs[i, 0:cols] = s.kappa[2 * i] + s.kappa[2 * i + 1]

    s.pairs[...] = jnp.zeros_like(s.pairs)
    kappa1 = restrict0(pair_of_kappa)
    s.kappa1[...] = kappa1
    s.k1[5 : 5 + mid_rows, 0:mid_cols] = kappa1[:, 0:mid_cols]
    m4 = copies(18, SIDES, lambda dh, da: s.kappa1, lambda dh, da: s.m4_in.at[0 if da == 1 else 1])
    me = copies(20, ENDS, lambda dh, da: layers_of(s.kappa1, dh, 5), lambda dh, da: s.me_in.at[end(dh)])
    mc = copies(22, CORNERS, lambda dh, da: layers_of(s.kappa1, dh, 4), lambda dh, da: s.mc_in.at[corner(dh, da)])

    def spread(packed, blocks, send_sem, recv_sem, kept):
        kept[...] = packed
        made = []
        for dh, da in far:
            copy = pltpu.make_async_remote_copy(
                src_ref=kept,
                dst_ref=blocks.at[(REACH - da) * n_ht + ht],
                send_sem=send_sem,
                recv_sem=recv_sem,
                device_id=far_device(dh, da),
                device_id_type=MESH,
            )
            copy.start()
        blocks[REACH * n_ht + ht] = packed

    def all_of(blocks, sem):
        some = blocks.at[0 : len(far)]
        return pltpu.make_async_copy(some, some, sem)

    spread(restrict1(kappa1), s.k2_blocks, s.far_send.at[0], s.far_recv.at[0], s.kappa2)

    def arrived(made, place):
        for (dh, da), copy in made.items():

            def take(dh=dh, da=da, copy=copy):
                copy.wait_recv()
                place(dh, da)

            there(-dh, take)

    def height(dh, layers, halo, size):
        return slice(halo - layers, halo) if dh == 1 else slice(halo + size, halo + size + layers)

    def place_k4(dh, da):
        low = 20 if da == 1 else cols
        s.k0[5 : 5 + rows, low : low + 4] = s.k4_in[0 if da == 1 else 1]

    def place_k5(dh, da):
        low = 19 if da == 1 else cols + 4
        s.k0[5 : 5 + rows, low : low + 1] = s.k5_in[0 if da == 1 else 1]

    def place_ke(dh, da):
        s.k0[height(dh, 5, 5, rows), 0:cols] = s.ke_in[end(dh)]

    def place_kc(dh, da):
        low = 20 if da == 1 else cols
        s.k0[height(dh, 4, 5, rows), low : low + 4] = s.kc_in[corner(dh, da)]

    arrived(k4, place_k4)
    arrived(k5, place_k5)
    arrived(ke, place_ke)
    arrived(kc, place_kc)

    fine = Level((s.k0, s.b0, s.x0, s.y0, s.d0, s.up0, s.side0, s.out0, s.inv0, s.piv0), 1.0, smooth_low, DEGREE)
    fine.set_up(jnp.where(has[-1], 0, 4), jnp.where(has[1], rows + 8, rows + 4), 2)

    def place_b4(dh, da):
        low = 20 if da == 1 else cols
        s.b0[4 : 4 + rows, low : low + 4] = s.b4_in[0 if da == 1 else 1]

    def place_be(dh, da):
        s.b0[height(dh, 4, 4, rows), 0:cols] = s.be_in[end(dh)]

    def place_bc(dh, da):
        low = 20 if da == 1 else cols
        s.b0[height(dh, 3, 4, rows), low : low + 4] = s.bc_in[corner(dh, da)]

    arrived(b4, place_b4)
    arrived(be, place_be)
    arrived(bc, place_bc)
    fine.smooth(2)

    def pair_of_residual(i):
        pair = fine.residual(4 + 2 * i) + fine.residual(5 + 2 * i)
        s.pairs[i] = pair[0:16]

    b1 = restrict0(pair_of_residual)
    s.source1[...] = b1
    s.b1[4 : 4 + mid_rows, 0:mid_cols] = b1[:, 0:mid_cols]
    s.n4_out[0] = b1[:, mid_cols - 4 : mid_cols]
    s.n4_out[1] = b1[:, 0:4]
    n4 = copies(26, SIDES, lambda dh, da: pick(s.n4_out, dh, da, 0, 0), lambda dh, da: s.n4_in.at[0 if da == 1 else 1])
    ne = copies(28, ENDS, lambda dh, da: layers_of(s.source1, dh, 4), lambda dh, da: s.ne_in.at[end(dh)])
    nc = copies(30, CORNERS, lambda dh, da: pick(s.n4_out, dh, da, 3, mid_rows), lambda dh, da: s.nc_in.at[corner(dh, da)])

    def place_m4(dh, da):
        if da == 1:
            s.k1[5 : 5 + mid_rows, 11:16] = s.m4_in[0, :, mid_cols - 5 : mid_cols]
        else:
            s.k1[5 : 5 + mid_rows, 6:11] = s.m4_in[1, :, 0:5]

    def place_me(dh, da):
        s.k1[height(dh, 5, 5, mid_rows), 0:mid_cols] = s.me_in[end(dh), :, 0:mid_cols]

    def place_mc(dh, da):
        here = s.mc_in[corner(dh, da)]
        if da == 1:
            s.k1[height(dh, 4, 5, mid_rows), 12:16] = here[:, mid_cols - 4 : mid_cols]
        else:
            s.k1[height(dh, 4, 5, mid_rows), 6:10] = here[:, 0:4]

    arrived(m4, place_m4)
    arrived(me, place_me)
    arrived(mc, place_mc)
    middle = Level((s.k1, s.b1, s.x1, s.y1, s.d1, s.up1, s.side1, s.out1, s.inv1, s.piv1), 0.25, smooth_low, DEGREE)
    middle.set_up(jnp.where(has[-1], 0, 4), jnp.where(has[1], mid_rows + 8, mid_rows + 4), 4)

    def place_n4(dh, da):
        low = 12 if da == 1 else mid_cols
        s.b1[4 : 4 + mid_rows, low : low + 4] = s.n4_in[0 if da == 1 else 1]

    def place_ne(dh, da):
        s.b1[height(dh, 4, 4, mid_rows), 0:mid_cols] = s.ne_in[end(dh), :, 0:mid_cols]

    def place_nc(dh, da):
        low = 12 if da == 1 else mid_cols
        s.b1[height(dh, 3, 4, mid_rows), low : low + 4] = s.nc_in[corner(dh, da)]

    arrived(n4, place_n4)
    arrived(ne, place_ne)
    arrived(nc, place_nc)
    middle.smooth(2)
    r1 = [middle.residual(4 + i)[0:8] for i in range(mid_rows)]
    spread(restrict1(r1), s.b2_blocks, s.far_send.at[1], s.far_recv.at[1], s.source2)

    coarse_cols = mid_cols // 2

    def lay_out(blocks, field):
        for step in range(-REACH, REACH + 1):
            low = (step * coarse_cols + 16) % 16
            for t in range(n_ht):
                block = blocks[(REACH + step) * n_ht + t]
                field[1 + 2 * t, low : low + coarse_cols] = block[0:coarse_cols]
                field[2 + 2 * t, low : low + coarse_cols] = block[4 : 4 + coarse_cols]

    lane = lax.broadcasted_iota(jnp.int32, (16, 128), 1)
    front = lane < 64
    last_lane, first_lane = lane % 64 == 63, lane % 64 == 0

    def above(field, row, i):
        if i == 0:
            return field[row + 1]
        return pltpu.roll(jnp.where(front, field[row + 1], field[row - 1]), 64, 1)

    def below(field, row, i):
        if i == 1:
            return field[row - 1]
        return pltpu.roll(jnp.where(front, field[row + 1], field[row - 1]), 64, 1)

    all_of(s.k2_blocks, s.far_recv.at[0]).wait()
    lay_out(s.k2_blocks, s.k2)

    first, steps = chebyshev_steps(COARSE_SWEEPS, coarse_low)

    def coarse_set_up(t):
        for i in range(2):
            row = 1 + 2 * t + i
            up, down, side, out, piv = face_coefs(
                s.k2[row], below(s.k2, row, i), above(s.k2, row, i), 0.5 * 0.0625, last_lane, first_lane
            )
            s.up2[row], s.down2[row], s.side2[row], s.out2[row] = up, down, side, out
            s.inv2[row] = 1.0 / piv

    each_row(0, n_ht, 2, coarse_set_up)

    all_of(s.b2_blocks, s.far_recv.at[1]).wait()
    lay_out(s.b2_blocks, s.b2)

    for row in range(1, 1 + 2 * n_ht):
        s.x2[row] = s.b2[row] * s.inv2[row] * first
    x2, y2 = s.x2, s.y2
    for number, (keep, add) in enumerate(steps):

        def sweep(t):
            for i in range(2):
                row = 1 + 2 * t + i
                x = x2[row]
                total = s.b2[row] + s.up2[row] * above(x2, row, i) + s.down2[row] * below(x2, row, i)
                total = total + in_layer(x, s.side2[row], s.out2[row])
                d = keep * (s.d2[row] if number else x) + add * (total * s.inv2[row] - x)
                s.d2[row] = d
                y2[row] = x + d

        if number < len(steps) - 1:
            each_row(0, n_ht, 4, sweep)
        else:
            sweep(ht)
        x2, y2 = y2, x2

    own = jnp.concatenate([x2[1 + 2 * ht, 0:8], x2[2 + 2 * ht, 0:8]], axis=0)
    spread_out = [exact_dot(own, s.wide2a[...]), exact_dot(own, s.wide2b[...])]
    for h in range(mid_rows // 2):
        part = spread_out[h // 2][8 * (h % 2) : 8 * (h % 2) + 4]
        s.raised1[pl.ds(h * 8, 4, stride=2), :] = part
        s.raised1[pl.ds(h * 8 + 1, 4, stride=2), :] = part
    for h in range(mid_rows):
        part = middle.x[4 + h, 0:8] + s.raised1[(h // 2) * 8 : (h // 2) * 8 + 8]
        s.raised0[pl.ds(h * 16, 8, stride=2), :] = part
        s.raised0[pl.ds(h * 16 + 1, 8, stride=2), :] = part
    raised = exact_dot(s.raised0[...], s.wide1[...]).reshape(mid_rows, 16, -1)
    for h in range(mid_rows):
        part = raised[h, 0:cols]
        s.res[2 * h] = fine.x[4 + 2 * h, 0:cols] + part
        s.res[2 * h + 1] = fine.x[5 + 2 * h, 0:cols] + part
    store = pltpu.make_async_copy(s.res, res_hbm, s.load_sem.at[3])
    store.start()

    for dh, da, copy in sent:
        there(dh, copy.wait_send)
    all_of(s.k2_blocks, s.far_send.at[0]).wait()
    all_of(s.b2_blocks, s.far_send.at[1]).wait()
    store.wait()


class Scratch:
    pass


def scratch_shapes(rows, cols, lanes, n_ht):
    mid_rows, mid_lanes = rows // 2, lanes // 2
    blocks = (2 * REACH + 1) * n_ht
    fields = {
        "coef": (rows, cols, lanes),
        "rhs": (rows, cols, lanes),
        "kappa": (rows, cols, lanes),
        "res": (rows, cols, lanes),
        "k4_out": (2, rows, 4, lanes),
        "k4_in": (2, rows, 4, lanes),
        "k5_out": (2, rows, 1, lanes),
        "k5_in": (2, rows, 1, lanes),
        "ke_in": (2, 5, cols, lanes),
        "kc_in": (4, 4, 4, lanes),
        "b4_out": (2, rows, 4, lanes),
        "b4_in": (2, rows, 4, lanes),
        "be_in": (2, 4, cols, lanes),
        "bc_in": (4, 3, 4, lanes),
        "pairs": (mid_rows, 16, lanes),
        "halves": (mid_rows * 16, mid_lanes),
        "quarters": (mid_rows // 2 * 8, mid_lanes),
        "kappa1": (mid_rows, 8, mid_lanes),
        "m4_in": (2, mid_rows, 8, mid_lanes),
        "me_in": (2, 5, 8, mid_lanes),
        "mc_in": (4, 4, 8, mid_lanes),
        "source1": (mid_rows, 8, mid_lanes),
        "n4_out": (2, mid_rows, 4, mid_lanes),
        "n4_in": (2, mid_rows, 4, mid_lanes),
        "ne_in": (2, 4, 8, mid_lanes),
        "nc_in": (4, 3, 4, mid_lanes),
        "kappa2": (8, 128),
        "source2": (8, 128),
        "k2_blocks": (blocks, 8, 128),
        "b2_blocks": (blocks, 8, 128),
        "raised1": (mid_rows // 2 * 8, mid_lanes),
        "raised0": (mid_rows * 16, mid_lanes),
    }
    for level, (size, sub, width) in enumerate(
        [(rows, 24, lanes), (mid_rows, 16, mid_lanes), (2 * n_ht - 6, 16, 128)]
    ):
        fields[f"k{level}"] = (size + 10, sub, width)
        for name in ("b", "x", "y", "d", "up", "down", "side", "out", "inv", "piv"):
            fields[f"{name}{level}"] = (size + 8, sub, width)
    shapes = {name: pltpu.VMEM(shape, F32) for name, shape in fields.items()}
    shapes["kind"] = pltpu.VMEM((rows, cols, lanes), jnp.int32)
    shapes["down0"] = pltpu.VMEM((lanes, mid_lanes), BF16)
    shapes["down1"] = pltpu.VMEM((mid_lanes, 128), BF16)
    shapes["wide1"] = pltpu.VMEM((mid_lanes, lanes), BF16)
    shapes["wide2a"] = pltpu.VMEM((128, mid_lanes), BF16)
    shapes["wide2b"] = pltpu.VMEM((128, mid_lanes), BF16)
    shapes["load_sem"] = pltpu.SemaphoreType.DMA((4,))
    shapes["send_sem"] = pltpu.SemaphoreType.DMA((34,))
    shapes["recv_sem"] = pltpu.SemaphoreType.DMA((34,))
    shapes["far_send"] = pltpu.SemaphoreType.DMA((2,))
    shapes["far_recv"] = pltpu.SemaphoreType.DMA((2,))
    return shapes


def solution(mesh):
    n_ht, n_az = mesh.shape["ht"], mesh.shape["az"]

    def on_device(right_side, base_coef, cell_type):
        shapes = scratch_shapes(*right_side.shape, n_ht)

        def body(rhs, coef, kind, res, *refs):
            s = Scratch()
            for name, ref in zip(shapes, refs):
                setattr(s, name, ref)
            kernel(n_ht, n_az, rhs, coef, kind, res, s)

        return pl.pallas_call(
            body,
            out_shape=jax.ShapeDtypeStruct(right_side.shape, F32),
            in_specs=[pl.BlockSpec(memory_space=pl.ANY)] * 3,
            out_specs=pl.BlockSpec(memory_space=pl.ANY),
            scratch_shapes=list(shapes.values()),
            compiler_params=pltpu.CompilerParams(
                collective_id=0, has_side_effects=True, vmem_limit_bytes=40 * 1024 * 1024
            ),
        )(right_side, base_coef, cell_type)

    placed = P("ht", "az", None)
    return jax.shard_map(
        on_device, mesh=mesh, in_specs=(placed,) * 3, out_specs=placed, check_vma=False
    )
```

time: 377 us -> 54.2 us (0.14)
  starting transfers between devices: 266 us -> 0 us
  waiting for transfers between devices: 57.6 us -> 0 us
  Pallas kernels: 0 us -> 51.1 us
  local copies, waits for them, and re-layouts: 32.9 us -> 2.92 us
  other arithmetic: 17.2 us -> 0 us
    ppermute x64 -> x0, starting transfers between devices: 266 us -> none  [the longest x32 165 us: extended_2(): lax.ppermute(head, axis, [((i + 1) % count, i) for i in range(count)])]
    ppermute x64 -> x0, waiting for transfers between devices: 57.6 us -> none  [the longest x32 57.5 us: extended_2(): lax.ppermute(head, axis, [((i + 1) % count, i) for i in range(count)])]
    pallas_call x0 -> x1, Pallas kernels: none -> 51.1 us  [on_device(): pl.pallas_call(body, out_shape=jax.ShapeDtypeStruct(right_side.shape, F32...]
    reshape x7 -> x0, local copies, waits for them, and re-layouts: 30.3 us -> none  [the longest x3 29.5 us: restrict(): values.reshape(shape[0] // 2, 2, shape[1] // 2, 2, shape[2] // 2, 2)]
    reduce_sum x4 -> x0, other arithmetic: 11.4 us -> none  [restrict(): return blocks.mean(axis=(1, 3, 5))]
  transfers between devices with their start and end apart: 64 -> 0, of which waited for: 22 -> 0; matrix products, arithmetic and copies ran while one was open for 6% -> 0% of each run, Pallas kernels for 0% -> 0%
where the time goes in v1:
time: 54.2 us; the launch traced here: 54 us
  Pallas kernels  51.1 us (94%)
  local copies, waits for them, and re-layouts  2.92 us (5%)
    pallas_call x1, Pallas kernels, on_device(): pl.pallas_call(body, out_shape=jax.ShapeDtypeStruct(right_side.shape, F32...  51.1 us
    unnamed x7, local copies, waits for them, and re-layouts  2.12 us

profile of v1, /device:TPU:1, one launch (start us, length us, event | category | flops | bytes accessed | tf_op | source)
XLA Modules:
  0.0 54.0 jit_solution(17784784575550092954)
XLA Ops:
  0.0 0.0 copy-start
  0.0 1.1 %copy.4.rhs = f32[16,12,256]{2,1,0:T(8,128)S(1)} copy(f32[16,12,256]{2,0,1:T(8,128)} %param.3) | data formatting | bytes 393216 | tf_op args[0]
  1.1 0.0 copy-done
  1.1 0.0 copy-start.1
  1.1 0.1 copy.5.coef
  1.2 0.8 %copy-done.1 = s32[16,12,256]{2,0,1:T(8,128)S(1)} copy-done((s32[16,12,256]{2,0,1:T(8,128)S(1)}, s32[16,12,256]{2,0,1:T(8,128)}, u32[]{:S(2)}) %copy-start.1) | copy-done | bytes 196632
  2.0 0.1 copy.6.kind
  2.2 51.1 %shard_map.37 = f32[16,12,256]{2,1,0:T(8,128)S(1)} custom-call(f32[16,12,256]{2,1,0:T(8,128)S(1)} %copy.4.rhs, f32[16,12,256]{2,1,0:T(8,128)S(1)} %copy.5.coef, s32[16,12,256]{2,1,0:T(8,128)S(1)} %copy.6.kind), custom_call_target="tpu_custom_call" | custom-call | tf_op jit(solution)/shard_map/pallas_call | solution.py:579
  53.2 0.8 %copy.7 = f32[16,12,256]{2,0,1:T(8,128)} copy(f32[16,12,256]{2,1,0:T(8,128)S(1)} %shard_map.37) | data formatting | bytes 393216 | tf_op jit(solution)/shard_map/pallas_call | solution.py:579
Async XLA Ops:
  0.0 1.1 %copy-start = (f32[16,12,256]{2,0,1:T(8,128)S(1)}, f32[16,12,256]{2,0,1:T(8,128)}, u32[]{:S(2)}) copy-start(f32[16,12,256]{2,0,1:T(8,128)} %param.4) | copy-start | bytes 589828
  1.1 0.9 %copy-start.1 = (s32[16,12,256]{2,0,1:T(8,128)S(1)}, s32[16,12,256]{2,0,1:T(8,128)}, u32[]{:S(2)}) copy-start(s32[16,12,256]{2,0,1:T(8,128)} %param.5) | copy-start | bytes 589828

commit v2 on v0

v2 whole, which is shorter than its diff:
```python
import jax
import jax.numpy as jnp
from jax import lax
from jax.experimental import pallas as pl
from jax.experimental.pallas import tpu as pltpu
from jax.sharding import PartitionSpec as P

DEGREE = 4
COARSE_SWEEPS = 6

shift_value = 0.002
smooth_low = 0.3
coarse_low = 0.02
high_end = 2.0

F32 = jnp.float32
BF16 = jnp.bfloat16
MESH = pl.DeviceIdType.MESH

NEAR = [(1, 1), (1, -1), (1, 0), (-1, 1), (-1, -1), (-1, 0), (0, 1), (0, -1)]
REACH = 2


def chebyshev_steps(degree, low_end):
    middle = 0.5 * (high_end + low_end)
    spread = 0.5 * (high_end - low_end)
    sigma_ratio = middle / spread
    rho_now = 1.0 / sigma_ratio
    steps = []
    for _ in range(degree - 1):
        rho_next = 1.0 / (2.0 * sigma_ratio - rho_now)
        keep, add = rho_next * rho_now, 2.0 * rho_next / spread
        steps.append((1.0 + keep - add, keep, add))
        rho_now = rho_next
    return 1.0 / middle, steps


def exact_dot(values, weights):
    count = values.shape[0]
    high = values.astype(BF16)
    rest = values - high.astype(F32)
    mid = rest.astype(BF16)
    low = (rest - mid.astype(F32)).astype(BF16)
    pieces = jnp.concatenate([high, mid, low], axis=0)
    total = jnp.dot(pieces, weights, preferred_element_type=F32)
    return total[0:count] + total[count : 2 * count] + total[2 * count :]


def each_row(start, count, block, body):
    if block >= count:
        for i in range(count):
            body(start + i)
        return

    def step(i, carry):
        for j in range(block):
            body(start + i * block + j)
        return carry

    lax.fori_loop(0, count // block, step, 0)


def next_in(values, axis):
    return pltpu.roll(values, values.shape[axis] - 1, axis)


def last_in(values, axis):
    return pltpu.roll(values, 1, axis)


def iotas(shape):
    return lax.broadcasted_iota(jnp.int32, shape, 0), lax.broadcasted_iota(jnp.int32, shape, 1)


class Level:
    def __init__(self, s, level, own, spacing, low_end, degree):
        for name in ("k", "b", "x", "y", "up", "side", "out", "inv", "piv"):
            setattr(self, name, getattr(s, f"{name}{level}"))
        self.own_az, self.own_ht = own
        self.rows, self.sub, self.lanes = self.b.shape
        self.half = 0.5 * spacing
        self.first, self.steps = chebyshev_steps(degree, low_end)

    def clear(self):
        for field in (self.k, self.b):
            rest = field.at[:, self.own_ht :]
            rest[...] = jnp.zeros(rest.shape, F32)

    def set_up(self, block, below, above):
        sub, lane = iotas((self.sub, self.lanes))
        last_lane, first_lane = lane == self.lanes - 1, lane == 0
        top, bottom = sub == self.own_ht + 3, sub == self.own_ht + 4
        lost = ((sub >= self.own_ht) & (sub < self.own_ht + 4) & jnp.logical_not(above)) | (
            (sub >= self.own_ht + 4) & jnp.logical_not(below)
        )
        inside = jnp.where(lost, 0.0, 1.0).astype(F32)

        own, nearer = self.own_ht, iotas((8, self.lanes))[0] < 4

        def folded(i):
            halo = jnp.where(nearer, self.k[i, own : own + 8], self.k[i, own + 8 : own + 16])
            return jnp.concatenate([self.k[i, 0:own], halo], axis=0)

        def body(i):
            k = folded(i + 1)
            up = self.half * (k + folded(i + 2))
            down = self.half * (k + folded(i))
            fifth_up, fifth_down = self.k[i + 1, own + 4 : own + 5], self.k[i + 1, own + 11 : own + 12]
            side = self.half * (k + jnp.where(top, fifth_up, next_in(k, 0)))
            under = jnp.where(bottom, self.half * (k + fifth_down), last_in(side, 0))
            out = self.half * (k + jnp.where(last_lane, 0.0, next_in(k, 1)))
            back = jnp.where(first_lane, self.half * k, last_in(out, 1))
            piv = shift_value + (up + down + side + under + out + back)
            self.up[i], self.side[i], self.piv[i] = up, side, piv
            self.out[i] = jnp.where(last_lane, 0.0, out)
            self.inv[i] = inside / piv

        each_row(0, self.rows, block, body)

    def gathered(self, i):
        x, side, out = self.x[i], self.side[i], self.out[i]
        total = self.b[i] + self.up[i] * self.x[i + 1] + self.up[i - 1] * self.x[i - 1]
        total = total + (side * next_in(x, 0) + last_in(side * x, 0))
        return total + (out * next_in(x, 1) + last_in(out * x, 1)), x

    def smooth(self, blocks):
        def start(i):
            self.x[i] = self.b[i] * self.inv[i] * self.first

        each_row(0, self.rows, blocks[0], start)
        for number, (scale, keep, add) in enumerate(self.steps):

            def body(i):
                total, x = self.gathered(i)
                new = scale * x + add * (total * self.inv[i])
                self.y[i] = new - keep * self.y[i] if number else new

            each_row(number + 1, self.rows - 2 * (number + 1), blocks[number + 1], body)
            self.x, self.y = self.y, self.x

    def residual(self, i):
        total, x = self.gathered(i)
        return total - self.piv[i] * x


def span(step, layers, halo, own, here):
    if step == 0:
        return pl.ds(halo, own)
    if step == 1:
        return pl.ds(halo + own - layers if here else halo - layers, layers)
    return pl.ds(halo if here else halo + own, layers)


def span_up(step, layers, sub, own, here):
    if step == 0:
        return pl.ds(0, own)
    if step == 1:
        return pl.ds(own - layers if here else sub - layers, layers)
    return pl.ds(0 if here else own, layers)


def kernel(n_ht, n_az, rhs_hbm, coef_hbm, type_hbm, res, s):
    ht, az = lax.axis_index("ht"), lax.axis_index("az")
    has = {1: ht < n_ht - 1, -1: ht > 0}
    cols, rows, _ = rhs_hbm.shape
    mid_cols, mid_rows = cols // 2, rows // 2
    low_cols = mid_cols // 2
    fine = Level(s, 0, (cols, rows), 1.0, smooth_low, DEGREE)
    middle = Level(s, 1, (mid_cols, mid_rows), 0.25, smooth_low, DEGREE)

    def there(dh, run):
        if dh == 0:
            run()
        else:
            pl.when(has[dh])(run)

    loads = [
        pltpu.make_async_copy(coef_hbm, s.coef, s.load_sem.at[0]),
        pltpu.make_async_copy(type_hbm, s.kind, s.load_sem.at[1]),
        pltpu.make_async_copy(rhs_hbm, s.b0.at[pl.ds(4, cols), pl.ds(0, rows)], s.load_sem.at[2]),
    ]
    for load in loads:
        load.start()

    fine.clear()
    middle.clear()
    far = [
        (dh, da)
        for da in (2, -2, 1, -1, 0)
        for dh in (2, 1, 3, 0)[4 - n_ht :]
        if (dh, da) != (0, 0)
    ]

    def far_device(dh, da):
        return {"ht": lax.rem(ht + dh, n_ht), "az": lax.rem(az + (da + n_az), n_az)}

    barrier = pltpu.get_barrier_semaphore()
    met = [(dh, da) for dh, da in far if abs(da) < 2]
    for dh, da in met:
        pl.semaphore_signal(barrier, inc=1, device_id=far_device(dh, da), device_id_type=MESH)

    sent = []

    def grouped(copies, act):
        for dh in (1, -1, 0):
            group = [copy for step, copy in copies if step == dh]

            def run(group=group):
                for copy in group:
                    act(copy)

            there(dh, run)

    def exchange(slot, field, level, halo, layers, corner_layers):
        made = []
        for i, (dh, da) in enumerate(NEAR):
            deep = corner_layers if dh and da else layers

            def part(here):
                return field.at[
                    span(da, deep, halo, level.own_az, here),
                    span_up(dh, deep, field.shape[1], level.own_ht, here),
                ]

            copy = pltpu.make_async_remote_copy(
                src_ref=part(True),
                dst_ref=part(False),
                send_sem=s.send_sem.at[slot + i],
                recv_sem=s.recv_sem.at[slot + i],
                device_id={"ht": ht + dh, "az": lax.rem(az + (da + n_az), n_az)},
                device_id_type=MESH,
            )
            made.append((dh, copy))
        grouped(made, lambda copy: copy.start())
        sent.extend(made)
        return made

    def arrived(made):
        grouped([(-dh, copy) for dh, copy in made], lambda copy: copy.wait_recv())

    loads[0].wait()
    loads[1].wait()

    def conductivity(a):
        kind = s.kind[a]
        factor = jnp.where(kind == 0, 0.1, jnp.where(kind == 1, 0.4, 1.0)).astype(F32)
        s.k0[5 + a, 0:rows] = s.coef[a] * factor

    each_row(0, cols, 6, conductivity)
    loads[2].wait()
    pl.semaphore_wait(barrier, len(met))
    k_fine = exchange(0, s.k0, fine, 5, 5, 4)
    b_fine = exchange(8, s.b0, fine, 4, 4, 3)

    def as_weights(picked, value):
        return jnp.where(picked, value, 0.0).astype(BF16)

    i, j = iotas(s.down0.shape)
    s.down0[...] = as_weights(i // 2 == j, 0.125)
    i, j = iotas(s.down1.shape)
    s.down1[...] = as_weights(i // 2 == j % 64, 0.125)
    i, j = iotas(s.wide0.shape)
    s.wide0[...] = as_weights(i == j // 2, 1.0)
    i, j = iotas(s.wide1.shape)
    s.wide1[...] = as_weights(i == j // 2, 1.0)

    sub, lane = iotas((8, 128))
    front = lane < 64
    even = sub % 2 == 0

    def restrict0(pair):
        pairs = jnp.concatenate([pair(i) for i in range(mid_cols)], axis=0)
        s.halves[...] = exact_dot(pairs, s.down0[...])
        count = mid_cols * mid_rows
        means = s.halves[pl.ds(0, count, stride=2), :] + s.halves[pl.ds(1, count, stride=2), :]
        return means.reshape(mid_cols, mid_rows, -1)

    def restrict1(pair):
        sums = exact_dot(jnp.concatenate([pair(i) for i in range(low_cols)], axis=0), s.down1[...])
        packed = []
        for i in range(low_cols):
            mean = sums[8 * i : 8 * i + 8]
            mean = mean + next_in(mean, 0)
            mean = jnp.where(front, mean, pltpu.roll(mean, 4, 0))
            packed.append(jnp.where(sub == 1, next_in(mean, 0), mean))
        return packed

    def spread(kept, field, number):
        block = kept.at[:, pl.ds(0, 2)]

        def place(da):
            return field.at[pl.ds((REACH - da) * low_cols, low_cols), pl.ds(2 * ht, 2)]

        for dh, da in far:
            pltpu.make_async_remote_copy(
                src_ref=block,
                dst_ref=place(da),
                send_sem=s.far_send.at[number],
                recv_sem=s.far_recv.at[number],
                device_id=far_device(dh, da),
                device_id_type=MESH,
            ).start()
        pltpu.make_async_copy(block, place(0), s.far_recv.at[number]).start()

    def all_in(field, number):
        pltpu.make_async_copy(field, field, s.far_recv.at[number]).wait()

    kappa1 = restrict0(lambda i: s.k0[5 + 2 * i, 0:rows] + s.k0[6 + 2 * i, 0:rows])
    s.k1[5 : 5 + mid_cols, 0:mid_rows] = kappa1
    k_middle = exchange(16, s.k1, middle, 5, 5, 4)
    kappa2 = restrict1(lambda i: kappa1[2 * i] + kappa1[2 * i + 1])
    for i, block in enumerate(kappa2):
        s.kept_k[i] = block

    arrived(k_fine)
    fine.set_up(4, has[-1], has[1])
    arrived(b_fine)
    fine.smooth((10, 6, 4, 7))

    def pair_of_residual(i):
        pair = fine.residual(4 + 2 * i) + fine.residual(5 + 2 * i)
        s.pairs[i] = pair[0:rows]

    each_row(0, mid_cols, 3, pair_of_residual)
    s.b1[4 : 4 + mid_cols, 0:mid_rows] = restrict0(lambda i: s.pairs[i])
    b_middle = exchange(24, s.b1, middle, 4, 4, 3)
    spread(s.kept_k, s.k2, 0)

    arrived(k_middle)
    middle.set_up(7, has[-1], has[1])
    arrived(b_middle)
    middle.smooth((14, 12, 10, 8))
    r1 = [middle.residual(4 + i)[0:mid_rows] for i in range(mid_cols)]
    for i, block in enumerate(restrict1(lambda i: r1[2 * i] + r1[2 * i + 1])):
        s.kept_b[i] = block
    spread(s.kept_b, s.b2, 1)

    inner_last, inner_first = lane % 64 == 63, lane % 64 == 0
    top = (sub == 2 * n_ht - 1) & jnp.logical_not(front)
    bottom = (sub == 0) & front

    def up_and_down(x):
        ahead, behind = next_in(x, 0), last_in(x, 0)
        swapped = pltpu.roll(jnp.where(front, ahead, behind), 64, 1)
        return jnp.where(even, ahead, swapped), jnp.where(even, swapped, behind)

    all_in(s.k2, 0)
    half = 0.5 * 0.0625
    reach = low_cols * REACH
    for a in range(1, 2 * reach + low_cols - 1):
        k = s.k2[a]
        above, below = up_and_down(k)
        above = half * (k + jnp.where(top, 0.0, above))
        below = half * (k + jnp.where(bottom, 0.0, below))
        up = half * (k + s.k2[a + 1])
        down = half * (k + s.k2[a - 1])
        out = half * (k + jnp.where(inner_last, 0.0, next_in(k, 1)))
        back = jnp.where(inner_first, half * k, last_in(out, 1))
        s.inv2[a] = 1.0 / (shift_value + (up + down + above + below + out + back))
        s.up2[a] = up
        s.above2[a] = jnp.where(top, 0.0, above)
        s.below2[a] = jnp.where(bottom, 0.0, below)
        s.out2[a] = jnp.where(inner_last, 0.0, out)

    all_in(s.b2, 1)
    first, steps = chebyshev_steps(COARSE_SWEEPS, coarse_low)
    size = 2 * reach + low_cols
    x = [None] + [s.b2[a] * s.inv2[a] * first for a in range(1, size - 1)] + [None]
    before = [None] * size
    for number, (scale, keep, add) in enumerate(steps):
        new = [None] * size
        for a in range(number + 2, size - number - 2):
            above, below = up_and_down(x[a])
            total = s.b2[a] + s.up2[a] * x[a + 1] + s.up2[a - 1] * x[a - 1]
            total = total + (s.above2[a] * above + s.below2[a] * below)
            out = s.out2[a]
            total = total + (out * next_in(x[a], 1) + last_in(out * x[a], 1))
            new[a] = scale * x[a] + add * (total * s.inv2[a])
            if number:
                new[a] = new[a] - keep * before[a]
        x, before = new, x

    tiles = []
    for i in range(low_cols):
        mine = pltpu.roll(x[reach + i], lax.rem(2 * n_ht - 2 * ht, 2 * n_ht), 0)
        mine = jnp.where(sub // 2 % 2 == 0, mine[0:1], mine[1:2])
        tiles.append(jnp.where(sub < 4, mine, pltpu.roll(mine, 64, 1)))
    raised = exact_dot(jnp.concatenate(tiles, axis=0), s.wide1[...])
    parts = [
        middle.x[4 + i, 0:mid_rows] + raised[8 * (i // 2) : 8 * (i // 2) + 8] for i in range(mid_cols)
    ]
    parts = jnp.concatenate(parts, axis=0)
    count = mid_cols * mid_rows
    s.doubled[pl.ds(0, count, stride=2), :] = parts
    s.doubled[pl.ds(1, count, stride=2), :] = parts
    raised = exact_dot(s.doubled[...], s.wide0[...])
    for a in range(cols):
        res[a] = fine.x[4 + a, 0:rows] + raised[rows * (a // 2) : rows * (a // 2) + rows]

    grouped(sent, lambda copy: copy.wait_send())
    for number in range(2):
        pltpu.make_async_copy(s.tally, s.tally, s.far_send.at[number]).wait()


class Scratch:
    pass


def scratch_shapes(cols, rows, lanes, n_ht):
    mid_cols, mid_rows, mid_lanes = cols // 2, rows // 2, lanes // 2
    low_cols = mid_cols // 2
    others = (2 * REACH + 1) * n_ht - 1
    fields = {
        "coef": (cols, rows, lanes),
        "pairs": (mid_cols, rows, lanes),
        "halves": (mid_cols * rows, mid_lanes),
        "doubled": (mid_cols * rows, mid_lanes),
        "kept_k": (low_cols, 8, 128),
        "kept_b": (low_cols, 8, 128),
        "tally": (others * low_cols, 2, 128),
    }
    for level, (size, sub, width) in enumerate([(cols, rows + 8, lanes), (mid_cols, mid_rows + 8, mid_lanes)]):
        fields[f"k{level}"] = (size + 10, sub + 8, width)
        for name in ("b", "x", "y", "up", "side", "out", "inv", "piv"):
            fields[f"{name}{level}"] = (size + 8, sub, width)
    for name in ("k2", "b2", "up2", "above2", "below2", "out2", "inv2"):
        fields[name] = ((2 * REACH + 1) * low_cols, 2 * n_ht, 128)
    shapes = {name: pltpu.VMEM(shape, F32) for name, shape in fields.items()}
    shapes["kind"] = pltpu.VMEM((cols, rows, lanes), jnp.int32)
    shapes["down0"] = pltpu.VMEM((lanes, mid_lanes), BF16)
    shapes["down1"] = pltpu.VMEM((mid_lanes, 128), BF16)
    shapes["wide0"] = pltpu.VMEM((mid_lanes, lanes), BF16)
    shapes["wide1"] = pltpu.VMEM((128, mid_lanes), BF16)
    shapes["load_sem"] = pltpu.SemaphoreType.DMA((3,))
    shapes["send_sem"] = pltpu.SemaphoreType.DMA((32,))
    shapes["recv_sem"] = pltpu.SemaphoreType.DMA((32,))
    shapes["far_send"] = pltpu.SemaphoreType.DMA((2,))
    shapes["far_recv"] = pltpu.SemaphoreType.DMA((2,))
    return shapes


def solution(mesh):
    n_ht, n_az = mesh.shape["ht"], mesh.shape["az"]

    def on_device(right_side, base_coef, cell_type):
        blocks = [jnp.transpose(block, (1, 0, 2)) for block in (right_side, base_coef, cell_type)]
        shape = blocks[0].shape
        shapes = scratch_shapes(*shape, n_ht)

        def body(rhs, coef, kind, res, *refs):
            s = Scratch()
            for name, ref in zip(shapes, refs):
                setattr(s, name, ref)
            kernel(n_ht, n_az, rhs, coef, kind, res, s)

        result = pl.pallas_call(
            body,
            out_shape=pltpu.VMEM(shape, F32),
            in_specs=[pl.BlockSpec(memory_space=pltpu.HBM)] * 3,
            out_specs=pl.BlockSpec(memory_space=pltpu.VMEM),
            scratch_shapes=list(shapes.values()),
            compiler_params=pltpu.CompilerParams(
                collective_id=0, has_side_effects=True, vmem_limit_bytes=56 * 1024 * 1024
            ),
        )(*blocks)
        return jnp.transpose(result, (1, 0, 2))

    placed = P("ht", "az", None)
    return jax.shard_map(
        on_device, mesh=mesh, in_specs=(placed,) * 3, out_specs=placed, check_vma=False
    )
```

time: 377 us -> 45.5 us (0.12)
  starting transfers between devices: 266 us -> 0 us
  waiting for transfers between devices: 57.6 us -> 0 us
  Pallas kernels: 0 us -> 44.7 us
  local copies, waits for them, and re-layouts: 32.9 us -> 0.68 us
  other arithmetic: 17.2 us -> 0 us
    ppermute x64 -> x0, starting transfers between devices: 266 us -> none  [the longest x32 165 us: extended_2(): lax.ppermute(head, axis, [((i + 1) % count, i) for i in range(count)])]
    ppermute x64 -> x0, waiting for transfers between devices: 57.6 us -> none  [the longest x32 57.5 us: extended_2(): lax.ppermute(head, axis, [((i + 1) % count, i) for i in range(count)])]
    pallas_call x0 -> x1, Pallas kernels: none -> 44.7 us  [on_device(): pl.pallas_call(body, out_shape=pltpu.VMEM(shape, F32), in_specs=[pl.Block...]
    reshape x7 -> x0, local copies, waits for them, and re-layouts: 30.3 us -> none  [the longest x3 29.5 us: restrict(): values.reshape(shape[0] // 2, 2, shape[1] // 2, 2, shape[2] // 2, 2)]
    reduce_sum x4 -> x0, other arithmetic: 11.4 us -> none  [restrict(): return blocks.mean(axis=(1, 3, 5))]
  transfers between devices with their start and end apart: 64 -> 0, of which waited for: 22 -> 0; matrix products, arithmetic and copies ran while one was open for 6% -> 0% of each run, Pallas kernels for 0% -> 0%
where the time goes in v2:
time: 45.5 us; the launch traced here: 45.3 us
  Pallas kernels  44.7 us (98%)
  local copies, waits for them, and re-layouts  0.68 us (1%)
    pallas_call x1, Pallas kernels, on_device(): pl.pallas_call(body, out_shape=pltpu.VMEM(shape, F32), in_specs=[pl.Block...  44.7 us

profile of v2, /device:TPU:1, one launch (start us, length us, event | category | flops | bytes accessed | tf_op | source)
XLA Modules:
  0.0 45.3 jit_solution(4503244642896908940)
XLA Ops:
  0.0 44.7 %shard_map.37 = f32[12,16,256]{2,1,0:T(8,128)S(1)} custom-call(f32[12,16,256]{2,1,0:T(8,128)} %bitcast.5, f32[12,16,256]{2,1,0:T(8,128)} %bitcast.6, s32[12,16,256]{2,1,0:T(8,128)} %bitcast.7), custom_call_target="tpu_custom_call" | custom-call | tf_op jit(solution)/shard_map/pallas_call | solution.py:456
  44.7 0.7 %copy.5 = f32[16,12,256]{2,0,1:T(8,128)} copy(f32[16,12,256]{2,0,1:T(8,128)S(1)} %bitcast.4) | data formatting | bytes 393216

commit v3 on v2

--- a/solution.py
+++ b/solution.py
@@ -17,7 +17,10 @@
 BF16 = jnp.bfloat16
 MESH = pl.DeviceIdType.MESH
 
-NEAR = [(1, 1), (1, -1), (1, 0), (-1, 1), (-1, -1), (-1, 0), (0, 1), (0, -1)]
+SIDES = [(0, 1), (0, -1)]
+ENDS = [(1, 0), (-1, 0)]
+CORNERS = [(1, 1), (1, -1), (-1, 1), (-1, -1)]
+NEAR = SIDES + ENDS + CORNERS
 REACH = 2
 
 
@@ -46,18 +49,19 @@
     return total[0:count] + total[count : 2 * count] + total[2 * count :]
 
 
-def each_row(start, count, block, body):
-    if block >= count:
-        for i in range(count):
-            body(start + i)
-        return
-
-    def step(i, carry):
-        for j in range(block):
-            body(start + i * block + j)
-        return carry
-
-    lax.fori_loop(0, count // block, step, 0)
+def each_row(ranges, body):
+    for first, count, block in ranges:
+        if block >= count:
+            for i in range(count):
+                body(first + i)
+            continue
+
+        def step(i, carry, first=first, block=block):
+            for j in range(block):
+                body(first + i * block + j)
+            return carry
+
+        lax.fori_loop(0, count // block, step, 0)
 
 
 def next_in(values, axis):
@@ -86,7 +90,7 @@
             rest = field.at[:, self.own_ht :]
             rest[...] = jnp.zeros(rest.shape, F32)
 
-    def set_up(self, block, below, above):
+    def set_up(self, ranges, below, above):
         sub, lane = iotas((self.sub, self.lanes))
         last_lane, first_lane = lane == self.lanes - 1, lane == 0
         top, bottom = sub == self.own_ht + 3, sub == self.own_ht + 4
@@ -115,31 +119,39 @@
             self.out[i] = jnp.where(last_lane, 0.0, out)
             self.inv[i] = inside / piv
 
-        each_row(0, self.rows, block, body)
-
-    def gathered(self, i):
-        x, side, out = self.x[i], self.side[i], self.out[i]
-        total = self.b[i] + self.up[i] * self.x[i + 1] + self.up[i - 1] * self.x[i - 1]
+        each_row(ranges, body)
+
+    def gathered(self, field, i):
+        x, side, out = field[i], self.side[i], self.out[i]
+        total = self.b[i] + self.up[i] * field[i + 1] + self.up[i - 1] * field[i - 1]
         total = total + (side * next_in(x, 0) + last_in(side * x, 0))
         return total + (out * next_in(x, 1) + last_in(out * x, 1)), x
 
-    def smooth(self, blocks):
-        def start(i):
+    def start(self, ranges):
+        def body(i):
             self.x[i] = self.b[i] * self.inv[i] * self.first
 
-        each_row(0, self.rows, blocks[0], start)
-        for number, (scale, keep, add) in enumerate(self.steps):
-
-            def body(i):
-                total, x = self.gathered(i)
-                new = scale * x + add * (total * self.inv[i])
-                self.y[i] = new - keep * self.y[i] if number else new
-
-            each_row(number + 1, self.rows - 2 * (number + 1), blocks[number + 1], body)
-            self.x, self.y = self.y, self.x
+        each_row(ranges, body)
+
+    def sweep(self, number, ranges):
+        scale, keep, add = self.steps[number]
+        old, new = self.fields(number)
+
+        def body(i):
+            total, x = self.gathered(old, i)
+            value = scale * x + add * (total * self.inv[i])
+            new[i] = value - keep * new[i] if number else value
+
+        each_row(ranges, body)
+
+    def fields(self, number):
+        return (self.y, self.x) if number % 2 else (self.x, self.y)
+
+    def result(self):
+        return self.fields(len(self.steps))[0]
 
     def residual(self, i):
-        total, x = self.gathered(i)
+        total, x = self.gathered(self.result(), i)
         return total - self.piv[i] * x
 
 
@@ -174,6 +186,32 @@
         else:
             pl.when(has[dh])(run)
 
+    @pl.when(jnp.logical_not(has[1] & has[-1]))
+    def _():
+        fine.clear()
+        middle.clear()
+
+    s.k2[...] = jnp.zeros_like(s.k2)
+    s.b2[...] = jnp.zeros_like(s.b2)
+
+    def device(dh, da):
+        return {"ht": ht + dh, "az": lax.rem(az + (da + n_az), n_az)}
+
+    def grouped(copies, act):
+        for dh in (1, -1, 0):
+            group = [copy for step, copy in copies if step == dh]
+
+            def run(group=group):
+                for copy in group:
+                    act(copy)
+
+            there(dh, run)
+
+    barrier = pltpu.get_barrier_semaphore()
+    grouped(
+        [(dh, (dh, da)) for dh, da in CORNERS + ENDS + SIDES],
+        lambda step: pl.semaphore_signal(barrier, inc=1, device_id=device(*step), device_id_type=MESH),
+    )
     loads = [
         pltpu.make_async_copy(coef_hbm, s.coef, s.load_sem.at[0]),
         pltpu.make_async_copy(type_hbm, s.kind, s.load_sem.at[1]),
@@ -182,52 +220,25 @@
     for load in loads:
         load.start()
 
-    fine.clear()
-    middle.clear()
-    far = [
-        (dh, da)
-        for da in (2, -2, 1, -1, 0)
-        for dh in (2, 1, 3, 0)[4 - n_ht :]
-        if (dh, da) != (0, 0)
-    ]
-
-    def far_device(dh, da):
-        return {"ht": lax.rem(ht + dh, n_ht), "az": lax.rem(az + (da + n_az), n_az)}
-
-    barrier = pltpu.get_barrier_semaphore()
-    met = [(dh, da) for dh, da in far if abs(da) < 2]
-    for dh, da in met:
-        pl.semaphore_signal(barrier, inc=1, device_id=far_device(dh, da), device_id_type=MESH)
-
     sent = []
 
-    def grouped(copies, act):
-        for dh in (1, -1, 0):
-            group = [copy for step, copy in copies if step == dh]
-
-            def run(group=group):
-                for copy in group:
-                    act(copy)
-
-            there(dh, run)
-
-    def exchange(slot, field, level, halo, layers, corner_layers):
+    def exchange(slot, directions, field, level, halo, layers):
         made = []
-        for i, (dh, da) in enumerate(NEAR):
-            deep = corner_layers if dh and da else layers
+        for dh, da in directions:
 
             def part(here):
                 return field.at[
-                    span(da, deep, halo, level.own_az, here),
-                    span_up(dh, deep, field.shape[1], level.own_ht, here),
+                    span(da, layers, halo, level.own_az, here),
+                    span_up(dh, layers, field.shape[1], level.own_ht, here),
                 ]
 
+            number = slot + NEAR.index((dh, da))
             copy = pltpu.make_async_remote_copy(
                 src_ref=part(True),
                 dst_ref=part(False),
-                send_sem=s.send_sem.at[slot + i],
-                recv_sem=s.recv_sem.at[slot + i],
-                device_id={"ht": ht + dh, "az": lax.rem(az + (da + n_az), n_az)},
+                send_sem=s.send_sem.at[number],
+                recv_sem=s.recv_sem.at[number],
+                device_id=device(dh, da),
                 device_id_type=MESH,
             )
             made.append((dh, copy))
@@ -246,11 +257,16 @@
         factor = jnp.where(kind == 0, 0.1, jnp.where(kind == 1, 0.4, 1.0)).astype(F32)
         s.k0[5 + a, 0:rows] = s.coef[a] * factor
 
-    each_row(0, cols, 6, conductivity)
+    each_row([(0, cols, 6)], conductivity)
+    ends = jnp.where(has[1], 1, 0) + jnp.where(has[-1], 1, 0)
+    pl.semaphore_wait(barrier, 2 + 3 * ends)
+    k_sides = exchange(0, CORNERS, s.k0, fine, 5, 4)
+    k_ends = exchange(0, ENDS, s.k0, fine, 5, 5)
+    k_sides += exchange(0, SIDES, s.k0, fine, 5, 5)
     loads[2].wait()
-    pl.semaphore_wait(barrier, len(met))
-    k_fine = exchange(0, s.k0, fine, 5, 5, 4)
-    b_fine = exchange(8, s.b0, fine, 4, 4, 3)
+    b_sides = exchange(8, CORNERS, s.b0, fine, 4, 3)
+    b_ends = exchange(8, ENDS, s.b0, fine, 4, 4)
+    b_sides += exchange(8, SIDES, s.b0, fine, 4, 4)
 
     def as_weights(picked, value):
         return jnp.where(picked, value, 0.0).astype(BF16)
@@ -285,55 +301,92 @@
             packed.append(jnp.where(sub == 1, next_in(mean, 0), mean))
         return packed
 
-    def spread(kept, field, number):
+    def spread(kept, field, first, groups):
         block = kept.at[:, pl.ds(0, 2)]
+
+        def there_far(dh, run):
+            if abs(dh) < 2:
+                there(dh, run)
+            else:
+                pl.when((ht + dh >= 0) & (ht + dh < n_ht))(run)
 
         def place(da):
             return field.at[pl.ds((REACH - da) * low_cols, low_cols), pl.ds(2 * ht, 2)]
 
-        for dh, da in far:
-            pltpu.make_async_remote_copy(
-                src_ref=block,
-                dst_ref=place(da),
-                send_sem=s.far_send.at[number],
-                recv_sem=s.far_recv.at[number],
-                device_id=far_device(dh, da),
-                device_id_type=MESH,
-            ).start()
-        pltpu.make_async_copy(block, place(0), s.far_recv.at[number]).start()
-
-    def all_in(field, number):
-        pltpu.make_async_copy(field, field, s.far_recv.at[number]).wait()
+        for number, (dh, reached) in enumerate(groups, first):
+
+            def go(dh=dh, reached=reached, number=number):
+                for da in reached:
+                    pltpu.make_async_remote_copy(
+                        src_ref=block,
+                        dst_ref=place(da),
+                        send_sem=s.far_send.at[number],
+                        recv_sem=s.far_recv.at[number],
+                        device_id=device(dh, da),
+                        device_id_type=MESH,
+                    ).start()
+
+            there_far(dh, go)
+        own = pltpu.make_async_copy(block, place(0), s.own_sem.at[first // len(groups)])
+        own.start()
+
+        def finish(towards, sems):
+            for number, (dh, reached) in enumerate(groups, first):
+                some = s.tally.at[pl.ds(0, len(reached) * low_cols)]
+
+                def wait(number=number, some=some):
+                    pltpu.make_async_copy(some, some, sems.at[number]).wait()
+
+                there_far(towards * dh, wait)
+            if towards < 0:
+                own.wait()
+
+        return finish
 
     kappa1 = restrict0(lambda i: s.k0[5 + 2 * i, 0:rows] + s.k0[6 + 2 * i, 0:rows])
     s.k1[5 : 5 + mid_cols, 0:mid_rows] = kappa1
-    k_middle = exchange(16, s.k1, middle, 5, 5, 4)
+    k_middle = exchange(16, CORNERS, s.k1, middle, 5, 4)
+    k_middle += exchange(16, ENDS + SIDES, s.k1, middle, 5, 5)
     kappa2 = restrict1(lambda i: kappa1[2 * i] + kappa1[2 * i + 1])
     for i, block in enumerate(kappa2):
         s.kept_k[i] = block
 
-    arrived(k_fine)
-    fine.set_up(4, has[-1], has[1])
-    arrived(b_fine)
-    fine.smooth((10, 6, 4, 7))
+    last = fine.rows
+    arrived(k_ends)
+    fine.set_up([(5, cols - 2, 5)], has[-1], has[1])
+    arrived(k_sides)
+    fine.set_up([(0, 5, 5), (last - 5, 5, 5)], has[-1], has[1])
+    arrived(b_ends)
+    fine.start([(4, cols, 6)])
+    for number, block in enumerate((5, 4, 6)):
+        fine.sweep(number, [(5 + number, cols - 2 - 2 * number, block)])
+    arrived(b_sides)
+    fine.start([(0, 4, 4), (last - 4, 4, 4)])
+    for number in range(len(fine.steps)):
+        fine.sweep(number, [(1 + number, 4, 4), (last - 5 - number, 4, 4)])
 
     def pair_of_residual(i):
         pair = fine.residual(4 + 2 * i) + fine.residual(5 + 2 * i)
         s.pairs[i] = pair[0:rows]
 
-    each_row(0, mid_cols, 3, pair_of_residual)
+    each_row([(0, mid_cols, 3)], pair_of_residual)
     s.b1[4 : 4 + mid_cols, 0:mid_rows] = restrict0(lambda i: s.pairs[i])
-    b_middle = exchange(24, s.b1, middle, 4, 4, 3)
-    spread(s.kept_k, s.k2, 0)
+    b_middle = exchange(24, CORNERS, s.b1, middle, 4, 3)
+    b_middle += exchange(24, ENDS + SIDES, s.b1, middle, 4, 4)
+    around = [2, -2, 1, -1]
+    k_coarse = spread(s.kept_k, s.k2, 0, [(1, around + [0]), (-1, around + [0]), (2, [1, -1, 0]), (-2, [1, -1, 0]), (0, around)])
 
     arrived(k_middle)
-    middle.set_up(7, has[-1], has[1])
+    middle.set_up([(0, middle.rows, 7)], has[-1], has[1])
     arrived(b_middle)
-    middle.smooth((14, 12, 10, 8))
+    middle.start([(0, middle.rows, middle.rows)])
+    for number in range(len(middle.steps)):
+        count = middle.rows - 2 - 2 * number
+        middle.sweep(number, [(1 + number, count, count)])
     r1 = [middle.residual(4 + i)[0:mid_rows] for i in range(mid_cols)]
     for i, block in enumerate(restrict1(lambda i: r1[2 * i] + r1[2 * i + 1])):
         s.kept_b[i] = block
-    spread(s.kept_b, s.b2, 1)
+    b_coarse = spread(s.kept_b, s.b2, 5, [(1, around + [0]), (-1, around + [0]), (2, [0]), (-2, [0]), (0, around)])
 
     inner_last, inner_first = lane % 64 == 63, lane % 64 == 0
     top = (sub == 2 * n_ht - 1) & jnp.logical_not(front)
@@ -344,7 +397,7 @@
         swapped = pltpu.roll(jnp.where(front, ahead, behind), 64, 1)
         return jnp.where(even, ahead, swapped), jnp.where(even, swapped, behind)
 
-    all_in(s.k2, 0)
+    k_coarse(-1, s.far_recv)
     half = 0.5 * 0.0625
     reach = low_cols * REACH
     for a in range(1, 2 * reach + low_cols - 1):
@@ -362,7 +415,7 @@
         s.below2[a] = jnp.where(bottom, 0.0, below)
         s.out2[a] = jnp.where(inner_last, 0.0, out)
 
-    all_in(s.b2, 1)
+    b_coarse(-1, s.far_recv)
     first, steps = chebyshev_steps(COARSE_SWEEPS, coarse_low)
     size = 2 * reach + low_cols
     x = [None] + [s.b2[a] * s.inv2[a] * first for a in range(1, size - 1)] + [None]
@@ -387,7 +440,7 @@
         tiles.append(jnp.where(sub < 4, mine, pltpu.roll(mine, 64, 1)))
     raised = exact_dot(jnp.concatenate(tiles, axis=0), s.wide1[...])
     parts = [
-        middle.x[4 + i, 0:mid_rows] + raised[8 * (i // 2) : 8 * (i // 2) + 8] for i in range(mid_cols)
+        middle.result()[4 + i, 0:mid_rows] + raised[8 * (i // 2) : 8 * (i // 2) + 8] for i in range(mid_cols)
     ]
     parts = jnp.concatenate(parts, axis=0)
     count = mid_cols * mid_rows
@@ -395,11 +448,11 @@
     s.doubled[pl.ds(1, count, stride=2), :] = parts
     raised = exact_dot(s.doubled[...], s.wide0[...])
     for a in range(cols):
-        res[a] = fine.x[4 + a, 0:rows] + raised[rows * (a // 2) : rows * (a // 2) + rows]
+        res[a] = fine.result()[4 + a, 0:rows] + raised[rows * (a // 2) : rows * (a // 2) + rows]
 
     grouped(sent, lambda copy: copy.wait_send())
-    for number in range(2):
-        pltpu.make_async_copy(s.tally, s.tally, s.far_send.at[number]).wait()
+    k_coarse(1, s.far_send)
+    b_coarse(1, s.far_send)
 
 
 class Scratch:
@@ -409,7 +462,6 @@
 def scratch_shapes(cols, rows, lanes, n_ht):
     mid_cols, mid_rows, mid_lanes = cols // 2, rows // 2, lanes // 2
     low_cols = mid_cols // 2
-    others = (2 * REACH + 1) * n_ht - 1
     fields = {
         "coef": (cols, rows, lanes),
         "pairs": (mid_cols, rows, lanes),
@@ -417,7 +469,7 @@
         "doubled": (mid_cols * rows, mid_lanes),
         "kept_k": (low_cols, 8, 128),
         "kept_b": (low_cols, 8, 128),
-        "tally": (others * low_cols, 2, 128),
+        "tally": ((2 * REACH + 1) * low_cols, 2, 128),
     }
     for level, (size, sub, width) in enumerate([(cols, rows + 8, lanes), (mid_cols, mid_rows + 8, mid_lanes)]):
         fields[f"k{level}"] = (size + 10, sub + 8, width)
@@ -434,8 +486,9 @@
     shapes["load_sem"] = pltpu.SemaphoreType.DMA((3,))
     shapes["send_sem"] = pltpu.SemaphoreType.DMA((32,))
     shapes["recv_sem"] = pltpu.SemaphoreType.DMA((32,))
-    shapes["far_send"] = pltpu.SemaphoreType.DMA((2,))
-    shapes["far_recv"] = pltpu.SemaphoreType.DMA((2,))
+    shapes["own_sem"] = pltpu.SemaphoreType.DMA((2,))
+    shapes["far_send"] = pltpu.SemaphoreType.DMA((10,))
+    shapes["far_recv"] = pltpu.SemaphoreType.DMA((10,))
     return shapes
 
 

time: 45.5 us -> 44 us (0.967)
  Pallas kernels: 44.7 us -> 43.2 us
    pallas_call x1, Pallas kernels: 44.7 us -> 43.2 us  [on_device(): pl.pallas_call(body, out_shape=pltpu.VMEM(shape, F32), in_specs=[pl.Block...]
where the time goes in v3:
time: 44 us; the launch traced here: 43.8 us
  Pallas kernels  43.2 us (98%)
  local copies, waits for them, and re-layouts  0.68 us (2%)
    pallas_call x1, Pallas kernels, on_device(): pl.pallas_call(body, out_shape=pltpu.VMEM(shape, F32), in_specs=[pl.Block...  43.2 us

profile of v3, /device:TPU:1, one launch (start us, length us, event | category | flops | bytes accessed | tf_op | source)
XLA Modules:
  0.0 43.8 jit_solution(7163344324784475709)
XLA Ops:
  0.0 43.2 %shard_map.37 = f32[12,16,256]{2,1,0:T(8,128)S(1)} custom-call(f32[12,16,256]{2,1,0:T(8,128)} %bitcast.5, f32[12,16,256]{2,1,0:T(8,128)} %bitcast.6, s32[12,16,256]{2,1,0:T(8,128)} %bitcast.7), custom_call_target="tpu_custom_call" | custom-call | tf_op jit(solution)/shard_map/pallas_call | solution.py:509
  43.2 0.7 %copy.5 = f32[16,12,256]{2,0,1:T(8,128)} copy(f32[16,12,256]{2,0,1:T(8,128)S(1)} %bitcast.4) | data formatting | bytes 393216

commit v4 on v3

--- a/solution.py
+++ b/solution.py
@@ -209,7 +209,7 @@
 
     barrier = pltpu.get_barrier_semaphore()
     grouped(
-        [(dh, (dh, da)) for dh, da in CORNERS + ENDS + SIDES],
+        [(dh, (dh, da)) for dh, da in ENDS + SIDES],
         lambda step: pl.semaphore_signal(barrier, inc=1, device_id=device(*step), device_id_type=MESH),
     )
     loads = [
@@ -259,13 +259,18 @@
 
     each_row([(0, cols, 6)], conductivity)
     ends = jnp.where(has[1], 1, 0) + jnp.where(has[-1], 1, 0)
-    pl.semaphore_wait(barrier, 2 + 3 * ends)
-    k_sides = exchange(0, CORNERS, s.k0, fine, 5, 4)
+    pl.semaphore_wait(barrier, 2 + ends)
+    grouped(
+        [(dh, (dh, da)) for dh, da in ENDS],
+        lambda step: pl.semaphore_signal(s.ready, inc=1, device_id=device(*step), device_id_type=MESH),
+    )
+    k_sides = exchange(0, SIDES, s.k0, fine, 5, 5)
     k_ends = exchange(0, ENDS, s.k0, fine, 5, 5)
-    k_sides += exchange(0, SIDES, s.k0, fine, 5, 5)
     loads[2].wait()
+    b_ends = exchange(8, ENDS, s.b0, fine, 4, 4)
+    pl.semaphore_wait(s.ready, ends)
+    k_sides += exchange(0, CORNERS, s.k0, fine, 5, 4)
     b_sides = exchange(8, CORNERS, s.b0, fine, 4, 3)
-    b_ends = exchange(8, ENDS, s.b0, fine, 4, 4)
     b_sides += exchange(8, SIDES, s.b0, fine, 4, 4)
 
     def as_weights(picked, value):
@@ -278,7 +283,7 @@
     i, j = iotas(s.wide0.shape)
     s.wide0[...] = as_weights(i == j // 2, 1.0)
     i, j = iotas(s.wide1.shape)
-    s.wide1[...] = as_weights(i == j // 2, 1.0)
+    s.wide1[...] = as_weights(i == j // 4, 1.0)
 
     sub, lane = iotas((8, 128))
     front = lane < 64
@@ -365,28 +370,38 @@
     for number in range(len(fine.steps)):
         fine.sweep(number, [(1 + number, 4, 4), (last - 5 - number, 4, 4)])
 
-    def pair_of_residual(i):
-        pair = fine.residual(4 + 2 * i) + fine.residual(5 + 2 * i)
-        s.pairs[i] = pair[0:rows]
-
-    each_row([(0, mid_cols, 3)], pair_of_residual)
-    s.b1[4 : 4 + mid_cols, 0:mid_rows] = restrict0(lambda i: s.pairs[i])
+    r0 = [fine.residual(4 + i)[0:rows] for i in range(cols)]
+    s.b1[4 : 4 + mid_cols, 0:mid_rows] = restrict0(lambda i: r0[2 * i] + r0[2 * i + 1])
     b_middle = exchange(24, CORNERS, s.b1, middle, 4, 3)
-    b_middle += exchange(24, ENDS + SIDES, s.b1, middle, 4, 4)
+    b_near = exchange(24, ENDS, s.b1, middle, 4, 4)
+    b_middle += exchange(24, SIDES, s.b1, middle, 4, 4)
     around = [2, -2, 1, -1]
     k_coarse = spread(s.kept_k, s.k2, 0, [(1, around + [0]), (-1, around + [0]), (2, [1, -1, 0]), (-2, [1, -1, 0]), (0, around)])
 
     arrived(k_middle)
     middle.set_up([(0, middle.rows, 7)], has[-1], has[1])
+    last = middle.rows
+    arrived(b_near)
+    middle.start([(4, mid_cols, mid_cols)])
+    for number in range(2):
+        middle.sweep(number, [(5 + number, mid_cols - 2 - 2 * number, mid_cols)])
     arrived(b_middle)
-    middle.start([(0, middle.rows, middle.rows)])
-    for number in range(len(middle.steps)):
-        count = middle.rows - 2 - 2 * number
-        middle.sweep(number, [(1 + number, count, count)])
+    middle.start([(0, 4, 4), (last - 4, 4, 4)])
+    for number in range(2):
+        middle.sweep(number, [(1 + number, 4, 4), (last - 5 - number, 4, 4)])
+    middle.sweep(2, [(3, last - 6, last)])
     r1 = [middle.residual(4 + i)[0:mid_rows] for i in range(mid_cols)]
     for i, block in enumerate(restrict1(lambda i: r1[2 * i] + r1[2 * i + 1])):
         s.kept_b[i] = block
     b_coarse = spread(s.kept_b, s.b2, 5, [(1, around + [0]), (-1, around + [0]), (2, [0]), (-2, [0]), (0, around)])
+
+    parts = middle.result()[4 : 4 + mid_cols, 0:mid_rows].reshape(mid_cols * mid_rows, -1)
+    count = mid_cols * mid_rows
+    s.doubled[pl.ds(0, count, stride=2), :] = parts
+    s.doubled[pl.ds(1, count, stride=2), :] = parts
+    raised = exact_dot(s.doubled[...], s.wide0[...])
+    for a in range(cols):
+        res[a] = fine.result()[4 + a, 0:rows] + raised[rows * (a // 2) : rows * (a // 2) + rows]
 
     inner_last, inner_first = lane % 64 == 63, lane % 64 == 0
     top = (sub == 2 * n_ht - 1) & jnp.logical_not(front)
@@ -436,19 +451,11 @@
     tiles = []
     for i in range(low_cols):
         mine = pltpu.roll(x[reach + i], lax.rem(2 * n_ht - 2 * ht, 2 * n_ht), 0)
-        mine = jnp.where(sub // 2 % 2 == 0, mine[0:1], mine[1:2])
-        tiles.append(jnp.where(sub < 4, mine, pltpu.roll(mine, 64, 1)))
+        mine = jnp.where(sub < 4, mine[0:1], mine[1:2])
+        tiles += [mine, pltpu.roll(mine, 64, 1)]
     raised = exact_dot(jnp.concatenate(tiles, axis=0), s.wide1[...])
-    parts = [
-        middle.result()[4 + i, 0:mid_rows] + raised[8 * (i // 2) : 8 * (i // 2) + 8] for i in range(mid_cols)
-    ]
-    parts = jnp.concatenate(parts, axis=0)
-    count = mid_cols * mid_rows
-    s.doubled[pl.ds(0, count, stride=2), :] = parts
-    s.doubled[pl.ds(1, count, stride=2), :] = parts
-    raised = exact_dot(s.doubled[...], s.wide0[...])
     for a in range(cols):
-        res[a] = fine.result()[4 + a, 0:rows] + raised[rows * (a // 2) : rows * (a // 2) + rows]
+        res[a] = res[a] + raised[rows * (a // 4) : rows * (a // 4) + rows]
 
     grouped(sent, lambda copy: copy.wait_send())
     k_coarse(1, s.far_send)
@@ -464,7 +471,6 @@
     low_cols = mid_cols // 2
     fields = {
         "coef": (cols, rows, lanes),
-        "pairs": (mid_cols, rows, lanes),
         "halves": (mid_cols * rows, mid_lanes),
         "doubled": (mid_cols * rows, mid_lanes),
         "kept_k": (low_cols, 8, 128),
@@ -482,11 +488,12 @@
     shapes["down0"] = pltpu.VMEM((lanes, mid_lanes), BF16)
     shapes["down1"] = pltpu.VMEM((mid_lanes, 128), BF16)
     shapes["wide0"] = pltpu.VMEM((mid_lanes, lanes), BF16)
-    shapes["wide1"] = pltpu.VMEM((128, mid_lanes), BF16)
+    shapes["wide1"] = pltpu.VMEM((128, lanes), BF16)
     shapes["load_sem"] = pltpu.SemaphoreType.DMA((3,))
     shapes["send_sem"] = pltpu.SemaphoreType.DMA((32,))
     shapes["recv_sem"] = pltpu.SemaphoreType.DMA((32,))
     shapes["own_sem"] = pltpu.SemaphoreType.DMA((2,))
+    shapes["ready"] = pltpu.SemaphoreType.REGULAR
     shapes["far_send"] = pltpu.SemaphoreType.DMA((10,))
     shapes["far_recv"] = pltpu.SemaphoreType.DMA((10,))
     return shapes

time: 44 us -> 43.3 us (0.984)
  Pallas kernels: 43.2 us -> 42.5 us
    pallas_call x1, Pallas kernels: 43.2 us -> 42.5 us  [on_device(): pl.pallas_call(body, out_shape=pltpu.VMEM(shape, F32), in_specs=[pl.Block...]
where the time goes in v4:
time: 43.3 us; the launch traced here: 43.1 us
  Pallas kernels  42.5 us (98%)
  local copies, waits for them, and re-layouts  0.68 us (2%)
    pallas_call x1, Pallas kernels, on_device(): pl.pallas_call(body, out_shape=pltpu.VMEM(shape, F32), in_specs=[pl.Block...  42.5 us

profile of v4, /device:TPU:1, one launch (start us, length us, event | category | flops | bytes accessed | tf_op | source)
XLA Modules:
  0.0 43.1 jit_solution(14784002995059591162)
XLA Ops:
  0.0 42.5 %shard_map.37 = f32[12,16,256]{2,1,0:T(8,128)S(1)} custom-call(f32[12,16,256]{2,1,0:T(8,128)} %bitcast.5, f32[12,16,256]{2,1,0:T(8,128)} %bitcast.6, s32[12,16,256]{2,1,0:T(8,128)} %bitcast.7), custom_call_target="tpu_custom_call" | custom-call | tf_op jit(solution)/shard_map/pallas_call | solution.py:516
  42.5 0.7 %copy.5 = f32[16,12,256]{2,0,1:T(8,128)} copy(f32[16,12,256]{2,0,1:T(8,128)S(1)} %bitcast.4) | data formatting | bytes 393216

commit v5 on v4

--- a/solution.py
+++ b/solution.py
@@ -350,21 +350,21 @@
 
     kappa1 = restrict0(lambda i: s.k0[5 + 2 * i, 0:rows] + s.k0[6 + 2 * i, 0:rows])
     s.k1[5 : 5 + mid_cols, 0:mid_rows] = kappa1
-    k_middle = exchange(16, CORNERS, s.k1, middle, 5, 4)
-    k_middle += exchange(16, ENDS + SIDES, s.k1, middle, 5, 5)
     kappa2 = restrict1(lambda i: kappa1[2 * i] + kappa1[2 * i + 1])
     for i, block in enumerate(kappa2):
         s.kept_k[i] = block
 
     last = fine.rows
     arrived(k_ends)
-    fine.set_up([(5, cols - 2, 5)], has[-1], has[1])
+    fine.set_up([(5, cols - 2, 10)], has[-1], has[1])
     arrived(k_sides)
     fine.set_up([(0, 5, 5), (last - 5, 5, 5)], has[-1], has[1])
     arrived(b_ends)
-    fine.start([(4, cols, 6)])
-    for number, block in enumerate((5, 4, 6)):
+    fine.start([(4, cols, 12)])
+    for number, block in enumerate((10, 8, 6)):
         fine.sweep(number, [(5 + number, cols - 2 - 2 * number, block)])
+    k_middle = exchange(16, CORNERS, s.k1, middle, 5, 4)
+    k_middle += exchange(16, ENDS + SIDES, s.k1, middle, 5, 5)
     arrived(b_sides)
     fine.start([(0, 4, 4), (last - 4, 4, 4)])
     for number in range(len(fine.steps)):
@@ -380,16 +380,11 @@
 
     arrived(k_middle)
     middle.set_up([(0, middle.rows, 7)], has[-1], has[1])
-    last = middle.rows
-    arrived(b_near)
-    middle.start([(4, mid_cols, mid_cols)])
-    for number in range(2):
-        middle.sweep(number, [(5 + number, mid_cols - 2 - 2 * number, mid_cols)])
-    arrived(b_middle)
-    middle.start([(0, 4, 4), (last - 4, 4, 4)])
-    for number in range(2):
-        middle.sweep(number, [(1 + number, 4, 4), (last - 5 - number, 4, 4)])
-    middle.sweep(2, [(3, last - 6, last)])
+    arrived(b_near + b_middle)
+    middle.start([(0, middle.rows, middle.rows)])
+    for number in range(len(middle.steps)):
+        count = middle.rows - 2 - 2 * number
+        middle.sweep(number, [(1 + number, count, count)])
     r1 = [middle.residual(4 + i)[0:mid_rows] for i in range(mid_cols)]
     for i, block in enumerate(restrict1(lambda i: r1[2 * i] + r1[2 * i + 1])):
         s.kept_b[i] = block

time: 43.3 us -> 42.9 us (level)
  no operation moved by 1% of the time
where the time goes in v5:
time: 42.9 us; the launch traced here: 42.8 us
  Pallas kernels  42.1 us (98%)
  local copies, waits for them, and re-layouts  0.68 us (2%)
    pallas_call x1, Pallas kernels, on_device(): pl.pallas_call(body, out_shape=pltpu.VMEM(shape, F32), in_specs=[pl.Block...  42.1 us

profile of v5, /device:TPU:1, one launch (start us, length us, event | category | flops | bytes accessed | tf_op | source)
XLA Modules:
  0.0 42.8 jit_solution(3773533531619680231)
XLA Ops:
  0.0 42.1 %shard_map.37 = f32[12,16,256]{2,1,0:T(8,128)S(1)} custom-call(f32[12,16,256]{2,1,0:T(8,128)} %bitcast.5, f32[12,16,256]{2,1,0:T(8,128)} %bitcast.6, s32[12,16,256]{2,1,0:T(8,128)} %bitcast.7), custom_call_target="tpu_custom_call" | custom-call | tf_op jit(solution)/shard_map/pallas_call | solution.py:511
  42.1 0.7 %copy.5 = f32[16,12,256]{2,0,1:T(8,128)} copy(f32[16,12,256]{2,0,1:T(8,128)S(1)} %bitcast.4) | data formatting | bytes 393216

commit v6 on v5

--- a/solution.py
+++ b/solution.py
@@ -267,10 +267,10 @@
     k_sides = exchange(0, SIDES, s.k0, fine, 5, 5)
     k_ends = exchange(0, ENDS, s.k0, fine, 5, 5)
     loads[2].wait()
-    b_ends = exchange(8, ENDS, s.b0, fine, 4, 4)
     pl.semaphore_wait(s.ready, ends)
     k_sides += exchange(0, CORNERS, s.k0, fine, 5, 4)
     b_sides = exchange(8, CORNERS, s.b0, fine, 4, 3)
+    b_ends = exchange(8, ENDS, s.b0, fine, 4, 4)
     b_sides += exchange(8, SIDES, s.b0, fine, 4, 4)
 
     def as_weights(picked, value):

time: 42.9 us -> 42.9 us (level)
  no operation moved by 1% of the time
where the time goes in v6:
time: 42.9 us; the launch traced here: 42.8 us
  Pallas kernels  42.1 us (98%)
  local copies, waits for them, and re-layouts  0.68 us (2%)
    pallas_call x1, Pallas kernels, on_device(): pl.pallas_call(body, out_shape=pltpu.VMEM(shape, F32), in_specs=[pl.Block...  42.1 us

profile of v6, /device:TPU:1, one launch (start us, length us, event | category | flops | bytes accessed | tf_op | source)
XLA Modules:
  0.0 42.8 jit_solution(7302369577136770035)
XLA Ops:
  0.0 42.1 %shard_map.37 = f32[12,16,256]{2,1,0:T(8,128)S(1)} custom-call(f32[12,16,256]{2,1,0:T(8,128)} %bitcast.5, f32[12,16,256]{2,1,0:T(8,128)} %bitcast.6, s32[12,16,256]{2,1,0:T(8,128)} %bitcast.7), custom_call_target="tpu_custom_call" | custom-call | tf_op jit(solution)/shard_map/pallas_call | solution.py:511
  42.1 0.7 %copy.5 = f32[16,12,256]{2,0,1:T(8,128)} copy(f32[16,12,256]{2,0,1:T(8,128)S(1)} %bitcast.4) | data formatting | bytes 393216
